TPU v7x, 256 devices: a whole 4x4x8 slice. The times are simulated.
256 devices in a mesh: gs: 64 (over x, z, core), view: 4 (over y).
Axes of the slice: x: 4, y: 4, z: 8, core: 2. Of those that a mesh axis runs over, the one named last changes fastest.
Arguments:
- sh_coef: float32 [48, 65536], P(None, 'gs'), may hold values from -4 to 4
- opacity_logit: float32 [65536], P('gs'), may hold values from -6 to -1
- view_angle: float32 [4, 2, 65536], P('view', None, 'gs'), may hold values from -3.140625 to 3.140625
- mean_pos: float32 [4, 2, 65536], P('view', None, 'gs'), may hold values from 0.15 to 0.85
- conic: float32 [4, 3, 65536], P('view', None, 'gs'), may hold values from -60 to 100, as said below
- send_slot: int32 [4, 65536], P('view', 'gs'), may hold values from 0 to 2047, as said below
- depth_rank: int32 [4, 65536], P('view', 'gs'), may hold values from 0 to 65535, each once within a row
- target: float32 [4, 256, 3, 1024], P('view', 'gs'), may hold values from 0 to 1
Outputs:
- sh_grad: float32 [48, 65536], P(None, 'gs')
- opacity_grad: float32 [65536], P('gs')
- mean_grad: float32 [4, 2, 65536], P('view', None, 'gs')
- rendered: float32 [4, 256, 3, 1024], P('view', 'gs')
Inputs may be any that keep to these rules, and one draw needn't show every extreme that they name: `send_slot`: in each view the 1024 values of one device's Gaussians are distinct, so no block holds more than 8 Gaussians of one device. In every view one block holds 8 Gaussians of every device, and every device fills some block's 8 places. `conic`: xx and yy lie in 8 to 100, and |xy| <= 0.6 sqrt(xx yy).
All inputs are finite; a program needn't handle non-finite values.
Results may differ from a plain program's by a relative error of at most 0.0003.
Values sent between devices are 32-bit elements; how exact they have to be, the bound alone decides.
A program may use at most 64 MiB of HBM per device.

v0:
```python
import jax
import jax.numpy as jnp
from jax import lax
from jax.sharding import PartitionSpec as P

TILE_PX = 16


SH_ZERO = 0.28209479177387814
SH_ONE = 0.4886025119029199
SH_TWO = (
    1.0925484305920792,
    -1.0925484305920792,
    0.31539156525252005,
    -1.0925484305920792,
    0.5462742152960396,
)
SH_THREE = (
    -0.5900435899266435,
    2.890611442640554,
    -0.4570457994644658,
    0.3731763325901154,
    -0.4570457994644658,
    1.445305721320277,
    -0.5900435899266435,
)
SSIM_MEAN = 0.0001
SSIM_SPREAD = 0.0009
HIGHEST = lax.Precision.HIGHEST


def unit_dirs(angles):
    polar = angles[0]
    azimuth = angles[1]
    return jnp.stack(
        [jnp.sin(polar) * jnp.cos(azimuth), jnp.sin(polar) * jnp.sin(azimuth), jnp.cos(polar)]
    )


def sh_basis(direction):
    coord_x, coord_y, coord_z = (direction[0], direction[1], direction[2])
    square_x = coord_x * coord_x
    square_y = coord_y * coord_y
    square_z = coord_z * coord_z
    terms = [
        SH_ZERO * jnp.ones_like(coord_x),
        -SH_ONE * coord_y,
        SH_ONE * coord_z,
        -SH_ONE * coord_x,
        SH_TWO[0] * coord_x * coord_y,
        SH_TWO[1] * coord_y * coord_z,
        SH_TWO[2] * (2.0 * square_z - square_x - square_y),
        SH_TWO[3] * coord_x * coord_z,
        SH_TWO[4] * (square_x - square_y),
        SH_THREE[0] * coord_y * (3.0 * square_x - square_y),
        SH_THREE[1] * coord_x * coord_y * coord_z,
        SH_THREE[2] * coord_y * (4.0 * square_z - square_x - square_y),
        SH_THREE[3] * coord_z * (2.0 * square_z - 3.0 * square_x - 3.0 * square_y),
        SH_THREE[4] * coord_x * (4.0 * square_z - square_x - square_y),
        SH_THREE[5] * coord_z * (square_x - square_y),
        SH_THREE[6] * coord_x * (square_x - 3.0 * square_y),
    ]
    return jnp.stack(terms)


def shade(coeffs, harmonics):
    return 0.5 + jnp.sum(coeffs.reshape(harmonics.shape[0], 3, -1) * harmonics[:, None, :], axis=0)


def pixel_grid(quad_side):
    pixels = jnp.arange(quad_side * quad_side, dtype=jnp.int32)
    across = ((pixels % quad_side).astype(jnp.float32) + 0.5) / quad_side
    downward = ((pixels // quad_side).astype(jnp.float32) + 0.5) / quad_side
    return (across, downward)


def render(colors, centers, conics, opacity, depth_order, across, downward):
    offset_u = across[None, :] - centers[0][:, None]
    offset_w = downward[None, :] - centers[1][:, None]
    quadratic = 0.5 * (
        conics[0][:, None] * offset_u * offset_u
        + 2.0 * conics[1][:, None] * offset_u * offset_w
        + conics[2][:, None] * offset_w * offset_w
    )
    alphas = opacity[:, None] * jnp.exp(-quadratic)
    before = (depth_order[None, :] < depth_order[:, None]).astype(jnp.float32)
    log_pass = jnp.dot(before, jnp.log1p(-alphas), precision=HIGHEST)
    weights = jnp.exp(log_pass) * alphas
    return jnp.dot(colors, weights, precision=HIGHEST)


def quad_loss(picture, target, quad_side):

    def block_mean(values):
        return values.reshape(3, quad_side // 4, 4, quad_side // 4, 4).mean(axis=(2, 4))

    difference = picture - target
    squared = jnp.sum(difference * difference) * (0.8 / 16.0)
    mean_x = block_mean(picture)
    mean_y = block_mean(target)
    spread_x = block_mean(picture * picture) - mean_x * mean_x
    spread_y = block_mean(target * target) - mean_y * mean_y
    joint = block_mean(picture * target) - mean_x * mean_y
    ssim_value = (
        (2.0 * mean_x * mean_y + SSIM_MEAN)
        * (2.0 * joint + SSIM_SPREAD)
        / ((mean_x * mean_x + mean_y * mean_y + SSIM_MEAN) * (spread_x + spread_y + SSIM_SPREAD))
    )
    return squared + 0.2 * jnp.sum(1.0 - ssim_value)


def quad_grads(colorize, coeffs, geometry, depth_order, target, across, downward, quad_side):

    def forward(coef_in, center_in, opacity_in):
        picture = render(
            colorize(coef_in), center_in, geometry[2:5], opacity_in, depth_order, across, downward
        )
        return (picture, quad_loss(picture, target, quad_side))

    (picture, loss_value), pullback = jax.vjp(forward, coeffs, geometry[0:2], geometry[5])
    grad_coef, grad_center, grad_opacity = pullback(
        (jnp.zeros_like(picture), jnp.ones_like(loss_value))
    )
    return (picture, jnp.concatenate([grad_coef, grad_center, grad_opacity[None]], axis=0))


def keep_colors(values):
    return values


def local(sh_coef, opacity_logit, view_angle, mean_pos, conic, send_slot, depth_rank, target):
    groups = lax.axis_size("gs")
    gauss_dev = sh_coef.shape[1]
    quads_dev = target.shape[1]
    place_cap = 2 * gauss_dev // (groups * quads_dev)
    block_rows = groups * place_cap
    quad_side = 2 * TILE_PX
    across, downward = pixel_grid(quad_side)
    harmonics = sh_basis(unit_dirs(view_angle[0]))
    sigmoid_value = jax.nn.sigmoid(opacity_logit)
    opacity = 0.99 * sigmoid_value
    slot_index = send_slot[0]
    block_index = slot_index // place_cap % quads_dev
    column = slot_index // (quads_dev * place_cap) * place_cap + slot_index % place_cap
    geometry = jnp.concatenate([mean_pos[0], conic[0], opacity[None]], axis=0)
    payload = jnp.concatenate([shade(sh_coef, harmonics), geometry], axis=0)
    width = payload.shape[0]
    buffer = (
        jnp.zeros((quads_dev, width, block_rows), jnp.float32)
        .at[block_index, :, column]
        .set(payload.T)
    )
    orders = (
        jnp.full((quads_dev, 1, block_rows), -1, jnp.int32)
        .at[block_index, 0, column]
        .set(depth_rank[0])
    )
    arrived, arrived_order = (
        lax.all_to_all(buffer, "gs", split_axis=2, concat_axis=2, tiled=True),
        lax.all_to_all(orders, "gs", split_axis=2, concat_axis=2, tiled=True),
    )

    def step_colors(inputs):
        rows_in, order_row, target_quad = inputs
        return quad_grads(
            keep_colors,
            rows_in[0:3],
            rows_in[3:9],
            order_row[0],
            target_quad,
            across,
            downward,
            quad_side,
        )

    images, grads = lax.map(step_colors, (arrived, arrived_order, target[0]))
    returned_all = lax.all_to_all(grads, "gs", split_axis=2, concat_axis=2, tiled=True)
    returned = returned_all[block_index, :, column].T
    slope = 0.99 * sigmoid_value * (1.0 - sigmoid_value)
    sh_part = (harmonics[:, None, :] * returned[0:3][None, :, :]).reshape(sh_coef.shape)
    logit_part = returned[-1] * slope
    sh_total, logit_total = lax.psum((sh_part, logit_part), "view")
    return (sh_total, logit_total, returned[-3:-1][None], images[None])


def solution(mesh):
    return jax.shard_map(
        local,
        mesh=mesh,
        in_specs=(
            P(None, "gs"),
            P("gs"),
            P("view", None, "gs"),
            P("view", None, "gs"),
            P("view", None, "gs"),
            P("view", "gs"),
            P("view", "gs"),
            P("view", "gs", None, None),
        ),
        out_specs=(P(None, "gs"), P("gs"), P("view", None, "gs"), P("view", "gs", None, None)),
        check_vma=False,
    )
```

profile of v0, /device:TPU:1, one launch (start us, length us, event | category | flops | bytes accessed | tf_op | source)
XLA Modules:
  0.0 226.9 jit_solution(3419134987301105390)
XLA Ops:
  7.2 0.8 shift-left_or_fusion
  7.9 0.7 and_reduce_fusion
  8.7 0.7 multiply_reduce_fusion.3
  9.4 4.5 %scatter_custom_fusion.1 = s32[2048]{0:T(1024)S(1)} fusion(s32[1024]{0:T(1024)S(1)} %broadcast_select_fusion, s32[1024]{0:T(1024)} %bitcast.242, s32[]{:T(128)} %constant.215.clone.1), kind=kCustom, calls=%fused_computation.168 | custom fusion | bytes 8704
  13.9 0.8 copy.49
  14.8 13.0 %all-to-all-start.1 = ((s32[4,1,512]{0,1,2:T(1,128)}), s32[4,1,512]{0,1,2:T(1,128)S(1)}, u32[]{:S(2)}, u32[]{:S(2)}) async-start(s32[4,1,512]{0,1,2:T(1,128)} %copy.49), calls=%async_computation.1 | async-start | bytes 524288 | tf_op jit(solution)/shard_map/all_to_all | solution.py:160
  27.8 1.0 bitcast_multiply_fusion.2
  28.8 0.8 multiply_bitcast_fusion
  29.6 0.9 bitcast_multiply_fusion.4
  30.5 0.7 and_reduce_fusion.1
  33.4 1.0 reshape.706
  35.6 3.3 %scatter_custom_fusion = f32[9,2048]{0,1:T(8,128)S(1)} fusion(s32[1024]{0:T(1024)S(1)} %broadcast_select_fusion.1, f32[1024,9]{1,0:T(8,128)S(1)} %copy.47, f32[]{:T(128)} %constant.211.clone.1), kind=kCustom, calls=%fused_computation.114 | custom fusion | bytes 73732
  39.7 2.0 reshape.759
  41.6 10.3 %all-to-all-start = ((f32[64,1,288]{2,1,0:T(1,128)}), f32[64,1,288]{2,1,0:T(1,128)S(1)}, u32[]{:S(2)}, u32[]{:S(2)}) async-start(f32[64,1,288]{2,1,0:T(1,128)} %reshape.759), calls=%async_computation | async-start | bytes 196608 | tf_op jit(solution)/shard_map/all_to_all | solution.py:159
  52.2 10.0 %all-to-all-done = f32[64,1,288]{2,1,0:T(1,128)S(1)} async-done(((f32[64,1,288]{2,1,0:T(1,128)}), f32[64,1,288]{2,1,0:T(1,128)S(1)}, u32[]{:S(2)}, u32[]{:S(2)}) %all-to-all-start) | async-done | bytes 73760 | tf_op jit(solution)/shard_map/all_to_all | solution.py:159
  62.7 0.9 reduce.10
  63.6 1.4 reshape.760
  65.3 87.1 %while.16 = (s32[]{:T(128)}, f32[4,3,1024]{2,0,1:T(4,128)S(1)}, f32[4,6,512]{2,1,0:T(8,128)S(1)}, f32[4,9,512]{2,1,0:T(8,128)S(1)}, s32[4,1,512]{2,1,0:T(1,128)S...) while((s32[]{:T(128)}, f32[4,3,1024]{2,0,1:T(4,128)S(1)}, ...), condition=%wide.region_12.13_spmd.clone, body=%wide.region_3.12_spmd.clone.sunk | while | flops 6550016000 | bytes 13277469 | solution.py:176
  65.6 3.7 %fusion.104 = f32[512,1024]{1,0:T(8,128)S(1)} fusion(f32[512]{0:T(512)S(1)} %bitcast.232, f32[512]{0:T(512)S(1)} %bitcast.216, f32[1024]{0:T(1024)S(1)} %get-tuple-element.292, f32[512]{0:T(512)S(1)} %bitcast.220, f32[512]{0:T(512)S(1)} %bitcast.224, f32[1024]{0:T(1024)S(1)} %get-tuple-element.295, f32[512]{0:T(512)S(1)} %bitcast.228, ...), kind=kOutput, calls=%fused_computation.34.clone.1 | convolution fusion | flops 3228827648 | bytes 2119680 | tf_op jit(solution)/shard_map/while/body/eval_jaxpr/jvp()/dot_general | solution.py:87
  69.3 2.5 %fusion.105 = f32[3,1024]{1,0:T(4,128)S(1)} fusion(f32[512,1024]{1,0:T(8,128)S(1)} %fusion.104, f32[512]{0:T(512)S(1)} %bitcast.233, f32[512]{0:T(512)S(1)} %bitcast.217, f32[1024]{0:T(1024)S(1)} %get-tuple-element.292, f32[512]{0:T(512)S(1)} %bitcast.221, f32[512]{0:T(512)S(1)} %bitcast.225, f32[1024]{0:T(1024)S(1)} %get-tuple-element.295, ...), kind=kOutput, calls=%fused_computation.51.clone.1 | convolution fusion | flops 26214400 | bytes 2138116 | tf_op jit(solution)/shard_map/while/body/eval_jaxpr/jvp()/dot_general | solution.py:89
  75.2 1.9 fusion.108
  77.1 6.9 %fusion.109 = (f32[512]{0:T(512)S(1)}, f32[512]{0:T(512)S(1)}, f32[512]{0:T(512)S(1)}) fusion(f32[512]{0:T(512)S(1)} %bitcast.234, f32[512]{0:T(512)S(1)} %bitcast.218, f32[1024]{0:T(1024)S(1)} %get-tuple-element.292, f32[512]{0:T(512)S(1)} %bitcast.222, f32[512]{0:T(512)S(1)} %bitcast.226, f32[1024]{0:T(1024)S(1)} %get-tuple-element.295, ...), kind=kOutput, calls=%fused_computation.18.clone.1 | convolution fusion | flops 3249797632 | bytes 4222976 | tf_op jit(solution)/shard_map/while/body/eval_jaxpr/transpose(jvp())/dot_general | solution.py:87
  84.0 3.1 %fusion.110 = f32[3,512]{1,0:T(4,128)S(1)} fusion(f32[3,1024]{1,0:T(4,128)S(1)} %add_add_fusion.5, f32[512,1024]{1,0:T(8,128)S(1)} %fusion.104, f32[512]{0:T(512)S(1)} %bitcast.235, f32[512]{0:T(512)S(1)} %bitcast.219, f32[1024]{0:T(1024)S(1)} %get-tuple-element.292, f32[512]{0:T(512)S(1)} %bitcast.223, f32[512]{0:T(512)S(1)} %bitcast.227, ...), kind=kOutput, calls=%fused_computation.50.clone.1 | convolution fusion | flops 26214400 | bytes 2136064 | tf_op jit(solution)/shard_map/while/body/eval_jaxpr/transpose(jvp())/dot_general | solution.py:89
  87.2 3.7 %fusion.104 = f32[512,1024]{1,0:T(8,128)S(1)} fusion(f32[512]{0:T(512)S(1)} %bitcast.232, f32[512]{0:T(512)S(1)} %bitcast.216, f32[1024]{0:T(1024)S(1)} %get-tuple-element.292, f32[512]{0:T(512)S(1)} %bitcast.220, f32[512]{0:T(512)S(1)} %bitcast.224, f32[1024]{0:T(1024)S(1)} %get-tuple-element.295, f32[512]{0:T(512)S(1)} %bitcast.228, ...), kind=kOutput, calls=%fused_computation.34.clone.1 | convolution fusion | flops 3228827648 | bytes 2119680 | tf_op jit(solution)/shard_map/while/body/eval_jaxpr/jvp()/dot_general | solution.py:87
  91.0 2.5 %fusion.105 = f32[3,1024]{1,0:T(4,128)S(1)} fusion(f32[512,1024]{1,0:T(8,128)S(1)} %fusion.104, f32[512]{0:T(512)S(1)} %bitcast.233, f32[512]{0:T(512)S(1)} %bitcast.217, f32[1024]{0:T(1024)S(1)} %get-tuple-element.292, f32[512]{0:T(512)S(1)} %bitcast.221, f32[512]{0:T(512)S(1)} %bitcast.225, f32[1024]{0:T(1024)S(1)} %get-tuple-element.295, ...), kind=kOutput, calls=%fused_computation.51.clone.1 | convolution fusion | flops 26214400 | bytes 2138116 | tf_op jit(solution)/shard_map/while/body/eval_jaxpr/jvp()/dot_general | solution.py:89
  96.9 1.9 fusion.108
  98.8 6.9 %fusion.109 = (f32[512]{0:T(512)S(1)}, f32[512]{0:T(512)S(1)}, f32[512]{0:T(512)S(1)}) fusion(f32[512]{0:T(512)S(1)} %bitcast.234, f32[512]{0:T(512)S(1)} %bitcast.218, f32[1024]{0:T(1024)S(1)} %get-tuple-element.292, f32[512]{0:T(512)S(1)} %bitcast.222, f32[512]{0:T(512)S(1)} %bitcast.226, f32[1024]{0:T(1024)S(1)} %get-tuple-element.295, ...), kind=kOutput, calls=%fused_computation.18.clone.1 | convolution fusion | flops 3249797632 | bytes 4222976 | tf_op jit(solution)/shard_map/while/body/eval_jaxpr/transpose(jvp())/dot_general | solution.py:87
  105.7 3.1 %fusion.110 = f32[3,512]{1,0:T(4,128)S(1)} fusion(f32[3,1024]{1,0:T(4,128)S(1)} %add_add_fusion.5, f32[512,1024]{1,0:T(8,128)S(1)} %fusion.104, f32[512]{0:T(512)S(1)} %bitcast.235, f32[512]{0:T(512)S(1)} %bitcast.219, f32[1024]{0:T(1024)S(1)} %get-tuple-element.292, f32[512]{0:T(512)S(1)} %bitcast.223, f32[512]{0:T(512)S(1)} %bitcast.227, ...), kind=kOutput, calls=%fused_computation.50.clone.1 | convolution fusion | flops 26214400 | bytes 2136064 | tf_op jit(solution)/shard_map/while/body/eval_jaxpr/transpose(jvp())/dot_general | solution.py:89
  108.9 3.7 %fusion.104 = f32[512,1024]{1,0:T(8,128)S(1)} fusion(f32[512]{0:T(512)S(1)} %bitcast.232, f32[512]{0:T(512)S(1)} %bitcast.216, f32[1024]{0:T(1024)S(1)} %get-tuple-element.292, f32[512]{0:T(512)S(1)} %bitcast.220, f32[512]{0:T(512)S(1)} %bitcast.224, f32[1024]{0:T(1024)S(1)} %get-tuple-element.295, f32[512]{0:T(512)S(1)} %bitcast.228, ...), kind=kOutput, calls=%fused_computation.34.clone.1 | convolution fusion | flops 3228827648 | bytes 2119680 | tf_op jit(solution)/shard_map/while/body/eval_jaxpr/jvp()/dot_general | solution.py:87
  112.7 2.5 %fusion.105 = f32[3,1024]{1,0:T(4,128)S(1)} fusion(f32[512,1024]{1,0:T(8,128)S(1)} %fusion.104, f32[512]{0:T(512)S(1)} %bitcast.233, f32[512]{0:T(512)S(1)} %bitcast.217, f32[1024]{0:T(1024)S(1)} %get-tuple-element.292, f32[512]{0:T(512)S(1)} %bitcast.221, f32[512]{0:T(512)S(1)} %bitcast.225, f32[1024]{0:T(1024)S(1)} %get-tuple-element.295, ...), kind=kOutput, calls=%fused_computation.51.clone.1 | convolution fusion | flops 26214400 | bytes 2138116 | tf_op jit(solution)/shard_map/while/body/eval_jaxpr/jvp()/dot_general | solution.py:89
  118.6 1.9 fusion.108
  120.4 6.9 %fusion.109 = (f32[512]{0:T(512)S(1)}, f32[512]{0:T(512)S(1)}, f32[512]{0:T(512)S(1)}) fusion(f32[512]{0:T(512)S(1)} %bitcast.234, f32[512]{0:T(512)S(1)} %bitcast.218, f32[1024]{0:T(1024)S(1)} %get-tuple-element.292, f32[512]{0:T(512)S(1)} %bitcast.222, f32[512]{0:T(512)S(1)} %bitcast.226, f32[1024]{0:T(1024)S(1)} %get-tuple-element.295, ...), kind=kOutput, calls=%fused_computation.18.clone.1 | convolution fusion | flops 3249797632 | bytes 4222976 | tf_op jit(solution)/shard_map/while/body/eval_jaxpr/transpose(jvp())/dot_general | solution.py:87
  127.4 3.1 %fusion.110 = f32[3,512]{1,0:T(4,128)S(1)} fusion(f32[3,1024]{1,0:T(4,128)S(1)} %add_add_fusion.5, f32[512,1024]{1,0:T(8,128)S(1)} %fusion.104, f32[512]{0:T(512)S(1)} %bitcast.235, f32[512]{0:T(512)S(1)} %bitcast.219, f32[1024]{0:T(1024)S(1)} %get-tuple-element.292, f32[512]{0:T(512)S(1)} %bitcast.223, f32[512]{0:T(512)S(1)} %bitcast.227, ...), kind=kOutput, calls=%fused_computation.50.clone.1 | convolution fusion | flops 26214400 | bytes 2136064 | tf_op jit(solution)/shard_map/while/body/eval_jaxpr/transpose(jvp())/dot_general | solution.py:89
  130.6 3.7 %fusion.104 = f32[512,1024]{1,0:T(8,128)S(1)} fusion(f32[512]{0:T(512)S(1)} %bitcast.232, f32[512]{0:T(512)S(1)} %bitcast.216, f32[1024]{0:T(1024)S(1)} %get-tuple-element.292, f32[512]{0:T(512)S(1)} %bitcast.220, f32[512]{0:T(512)S(1)} %bitcast.224, f32[1024]{0:T(1024)S(1)} %get-tuple-element.295, f32[512]{0:T(512)S(1)} %bitcast.228, ...), kind=kOutput, calls=%fused_computation.34.clone.1 | convolution fusion | flops 3228827648 | bytes 2119680 | tf_op jit(solution)/shard_map/while/body/eval_jaxpr/jvp()/dot_general | solution.py:87
  134.3 2.5 %fusion.105 = f32[3,1024]{1,0:T(4,128)S(1)} fusion(f32[512,1024]{1,0:T(8,128)S(1)} %fusion.104, f32[512]{0:T(512)S(1)} %bitcast.233, f32[512]{0:T(512)S(1)} %bitcast.217, f32[1024]{0:T(1024)S(1)} %get-tuple-element.292, f32[512]{0:T(512)S(1)} %bitcast.221, f32[512]{0:T(512)S(1)} %bitcast.225, f32[1024]{0:T(1024)S(1)} %get-tuple-element.295, ...), kind=kOutput, calls=%fused_computation.51.clone.1 | convolution fusion | flops 26214400 | bytes 2138116 | tf_op jit(solution)/shard_map/while/body/eval_jaxpr/jvp()/dot_general | solution.py:89
  140.2 1.9 fusion.108
  142.1 6.9 %fusion.109 = (f32[512]{0:T(512)S(1)}, f32[512]{0:T(512)S(1)}, f32[512]{0:T(512)S(1)}) fusion(f32[512]{0:T(512)S(1)} %bitcast.234, f32[512]{0:T(512)S(1)} %bitcast.218, f32[1024]{0:T(1024)S(1)} %get-tuple-element.292, f32[512]{0:T(512)S(1)} %bitcast.222, f32[512]{0:T(512)S(1)} %bitcast.226, f32[1024]{0:T(1024)S(1)} %get-tuple-element.295, ...), kind=kOutput, calls=%fused_computation.18.clone.1 | convolution fusion | flops 3249797632 | bytes 4222976 | tf_op jit(solution)/shard_map/while/body/eval_jaxpr/transpose(jvp())/dot_general | solution.py:87
  149.1 3.1 %fusion.110 = f32[3,512]{1,0:T(4,128)S(1)} fusion(f32[3,1024]{1,0:T(4,128)S(1)} %add_add_fusion.5, f32[512,1024]{1,0:T(8,128)S(1)} %fusion.104, f32[512]{0:T(512)S(1)} %bitcast.235, f32[512]{0:T(512)S(1)} %bitcast.219, f32[1024]{0:T(1024)S(1)} %get-tuple-element.292, f32[512]{0:T(512)S(1)} %bitcast.223, f32[512]{0:T(512)S(1)} %bitcast.227, ...), kind=kOutput, calls=%fused_computation.50.clone.1 | convolution fusion | flops 26214400 | bytes 2136064 | tf_op jit(solution)/shard_map/while/body/eval_jaxpr/transpose(jvp())/dot_general | solution.py:89
  152.9 1.4 reshape.761
  154.2 14.0 %all_to_all.15 = f32[64,1,192]{2,1,0:T(1,128)S(1)} all-to-all(f32[64,1,192]{2,1,0:T(1,128)S(1)} %reshape.761), channel_id=1, replica_groups=mesh['gs'=64,'view'=4] {'gs'}, dimensions={0} | all-to-all | bytes 98304 | tf_op jit(solution)/shard_map/all_to_all | solution.py:177
  168.2 0.8 reduce.11
  169.0 1.4 reshape.762
  170.4 6.8 %gather_fusion = f32[1024,6]{1,0:T(8,128)S(1)} fusion(f32[4,6,512]{1,2,0:T(8,128)S(1)} %copy.54, s32[1024]{0:T(1024)S(1)} %bitcast.198), kind=kCustom, calls=%fused_computation | custom fusion | bytes 57344 | tf_op jit(solution)/shard_map/gather | solution.py:178
  178.1 0.8 mul.1136
  178.9 0.8 copy.57
  179.7 9.7 %psum.15 = f32[1024]{0:T(1024)} all-reduce(f32[1024]{0:T(1024)S(1)} %multiply_multiply_fusion), channel_id=1, replica_groups=mesh['gs'=64,'view'=4] {'view'}, use_global_device_ids=true, to_apply=%region_14.15 | all-reduce | flops 1024 | bytes 8192 | tf_op jit(solution)/shard_map/psum | solution.py:182
  189.4 29.0 %all-reduce.4.cloned.1.call-done = f32[48,1024]{1,0:T(8,128)} async-done(((f32[48,1024]{1,0:T(8,128)}), f32[48,1024]{1,0:T(8,128)}) %all-reduce.4.cloned.1.call-update) | async-done | bytes 196624 | tf_op jit(solution)/shard_map/psum | solution.py:182
  218.4 1.6 copy.84
  (141 shorter events, 19.9 us)
Async XLA Ops:
  14.8 26.8 %all-to-all-start.1 = ((s32[4,1,512]{0,1,2:T(1,128)}), s32[4,1,512]{0,1,2:T(1,128)S(1)}, u32[]{:S(2)}, u32[]{:S(2)}) async-start(s32[4,1,512]{0,1,2:T(1,128)} %copy.49), calls=%async_computation.1 | async-start | bytes 524288 | tf_op jit(solution)/shard_map/all_to_all | solution.py:160
  35.6 16.4 %copy-start = (f32[1,4,3,1024]{3,1,2,0:T(4,128)S(1)}, f32[1,4,3,1024]{3,1,2,0:T(4,128)}, u32[]{:S(2)}) copy-start(f32[1,4,3,1024]{3,1,2,0:T(4,128)} %param.17) | copy-start | bytes 147460
  41.6 20.5 %all-to-all-start = ((f32[64,1,288]{2,1,0:T(1,128)}), f32[64,1,288]{2,1,0:T(1,128)S(1)}, u32[]{:S(2)}, u32[]{:S(2)}) async-start(f32[64,1,288]{2,1,0:T(1,128)} %reshape.759), calls=%async_computation | async-start | bytes 196608 | tf_op jit(solution)/shard_map/all_to_all | solution.py:159
  52.0 166.4 %all-reduce.4.cloned.1.call-start = ((), (), s32[]{:S(2)}) async-start(), calls=%async_computation.3 | async-start | bytes 393216 | tf_op jit(solution)/shard_map/psum | solution.py:182
  152.4 18.0 %copy-start.2 = (f32[4,3,1024]{2,0,1:T(4,128)}, f32[4,3,1024]{2,0,1:T(4,128)S(1)}, u32[]{:S(2)}) copy-start(f32[4,3,1024]{2,0,1:T(4,128)S(1)} %get-tuple-element.129) | copy-start | bytes 147460
  177.2 2.4 %copy-start.1 = (f32[1024]{0:T(1024)S(1)}, f32[1024]{0:T(1024)}, u32[]{:S(2)}) copy-start(f32[1024]{0:T(1024)} %param.11) | copy-start | bytes 12292
Sparse Core Ops, SparseCore 0:
  179.0 39.3 all-reduce.3
where the time goes:
time: 229 us; the launch traced here: 227 us
  matrix products  72.5 us (32%)
  local copies, waits for them, and re-layouts  40.7 us (18%)
  waiting for transfers between devices  39 us (17%)
  blocking collectives  23.6 us (10%)
  starting transfers between devices  23.3 us (10%)
  between operations  14.3 us (6%)
  other arithmetic  12.2 us (5%)
    dot_general x8, matrix products, render(): log_pass = jnp.dot(before, jnp.log1p(-alphas), precision=HIGHEST)  42.6 us
    dot_general x12, matrix products, render(): return jnp.dot(colors, weights, precision=HIGHEST)  29.9 us
    psum x1, waiting for transfers between devices, local(): sh_total, logit_total = lax.psum((sh_part, logit_part), 'view')  29 us
    unnamed x19, local copies, waits for them, and re-layouts  18.2 us
    all_to_all x1, blocking collectives, local(): lax.all_to_all(grads, 'gs', split_axis=2, concat_axis=2, tiled=True)  14 us
    all_to_all x1, starting transfers between devices, local(): lax.all_to_all(orders, 'gs', split_axis=2, concat_axis=2, tiled=True)  13 us
    all_to_all x1, starting transfers between devices, local(): lax.all_to_all(buffer, 'gs', split_axis=2, concat_axis=2, tiled=True)  10.3 us
    all_to_all x1, waiting for transfers between devices, local(): lax.all_to_all(buffer, 'gs', split_axis=2, concat_axis=2, tiled=True)  9.95 us
  transfers between devices with their start and end apart: 3, of which 2 were waited for; matrix products, arithmetic and copies ran while one was open for 6% of the time, Pallas kernels for 0%

commit v1 on v0

v1 whole, which is shorter than its diff:
```python
import jax
import jax.numpy as jnp
from jax import lax
from jax.experimental import pallas as pl
from jax.experimental.pallas import tpu as pltpu
from jax.sharding import PartitionSpec as P

F32 = jnp.float32
BF16 = jnp.bfloat16

SH_ZERO = 0.28209479177387814
SH_ONE = 0.4886025119029199
SH_TWO = (
    1.0925484305920792,
    -1.0925484305920792,
    0.31539156525252005,
    -1.0925484305920792,
    0.5462742152960396,
)
SH_THREE = (
    -0.5900435899266435,
    2.890611442640554,
    -0.4570457994644658,
    0.3731763325901154,
    -0.4570457994644658,
    1.445305721320277,
    -0.5900435899266435,
)
SSIM_MEAN = 0.0001
SSIM_SPREAD = 0.0009

GS = 64
VIEWS = 4
QUADS = 4
CAP = 8
G = 1024
PLACES = GS * CAP
PIX = 1024
TILES = PIX // 128
WIDE = 16
OPA, COL, KEY = 6, 7, 10
BACK = 8
HIGHEST = lax.Precision.HIGHEST


def iota(shape, axis):
    return lax.broadcasted_iota(jnp.int32, shape, axis)


def sh_basis(polar, azimuth):
    across = jnp.sin(polar)
    x = across * jnp.cos(azimuth)
    y = across * jnp.sin(azimuth)
    z = jnp.cos(polar)
    xx, yy, zz = x * x, y * y, z * z
    return [
        jnp.full_like(x, SH_ZERO),
        -SH_ONE * y,
        SH_ONE * z,
        -SH_ONE * x,
        SH_TWO[0] * x * y,
        SH_TWO[1] * y * z,
        SH_TWO[2] * (2.0 * zz - xx - yy),
        SH_TWO[3] * x * z,
        SH_TWO[4] * (xx - yy),
        SH_THREE[0] * y * (3.0 * xx - yy),
        SH_THREE[1] * x * y * z,
        SH_THREE[2] * y * (4.0 * zz - xx - yy),
        SH_THREE[3] * z * (2.0 * zz - 3.0 * xx - 3.0 * yy),
        SH_THREE[4] * x * (4.0 * zz - xx - yy),
        SH_THREE[5] * z * (xx - yy),
        SH_THREE[6] * x * (xx - 3.0 * yy),
    ]


def three_parts(values):
    high = values.astype(BF16).astype(F32)
    rest = values - high
    middle = rest.astype(BF16).astype(F32)
    return high, middle, rest - middle


def centre(mean):
    return mean * 32.0 - 16.5


def pack_kernel(sh_ref, logit_ref, angle_ref, mean_ref, conic_ref, slot_ref, rank_ref, out_ref, pay):
    basis = sh_basis(angle_ref[0:1, :], angle_ref[1:2, :])
    colour = jnp.full((3, G), 0.5, F32)
    for k in range(16):
        colour = colour + sh_ref[3 * k : 3 * k + 3, :] * basis[k]
    m, n = centre(mean_ref[0:1, :]), centre(mean_ref[1:2, :])
    scale = 1.0 / 1024.0
    a, b, c = (conic_ref[k : k + 1, :] * scale for k in range(3))
    pay[...] = jnp.zeros((WIDE, G), F32)
    pay[0:1, :] = -0.5 * (a * m * m + 2.0 * b * m * n + c * n * n)
    pay[1:2, :] = a * m + b * n
    pay[2:3, :] = b * m + c * n
    pay[3:4, :] = -0.5 * a
    pay[4:5, :] = -b
    pay[5:6, :] = -0.5 * c
    pay[OPA : OPA + 1, :] = 0.99 * jax.nn.sigmoid(logit_ref[...])
    pay[COL : COL + 3, :] = colour
    pay[KEY : KEY + 1, :] = (rank_ref[...] + 1).astype(F32)
    parts = three_parts(pay[...])
    slot = slot_ref[...]
    owner = jnp.where(iota((GS, G), 0) == (slot >> 5), 1.0, 0.0).astype(BF16)
    place = slot & 31
    for q in range(QUADS):
        total = jnp.zeros((GS, 128), F32)
        for part in parts[::-1]:
            spread = jnp.concatenate(
                [jnp.where(place == q * CAP + cap, part, 0.0) for cap in range(CAP)], axis=0
            ).astype(BF16)
            total = total + lax.dot_general(
                owner, spread, (((1,), (1,)), ((), ())), preferred_element_type=F32
            )
        out_ref[:, q, :] = total


def monomials():
    lane = iota((WIDE, 128), 1)
    row = iota((WIDE, 128), 0)
    u = ((lane & 31) - 16).astype(F32)
    w = ((lane >> 5) - 16).astype(F32)

    def rows(entries):
        out = jnp.zeros((WIDE, 128), F32)
        for k, value in entries.items():
            out = jnp.where(row == k, value, out)
        return out

    tiles = [
        rows({0: 1.0, 1: u, 2: w, 3: u * u, 4: u * w, 5: w * w}),
        rows({2: 4.0, 4: 4.0 * u, 5: 8.0 * w + 16.0}),
        rows({5: 32.0}),
        rows({OPA: 1.0}),
        rows({COL: 1.0}),
        rows({COL + 1: 1.0}),
        rows({COL + 2: 1.0}),
    ]
    base = jnp.concatenate(tiles, axis=1)
    pad = jnp.zeros((128 - 3 * WIDE, base.shape[1]), F32)
    return jnp.concatenate([base, base, base, pad], axis=0).astype(BF16)


def loss_slope(x, y):
    lane = iota((128, 128), 1)
    other = iota((128, 128), 0)
    same = ((lane & 31) >> 2) == ((other & 31) >> 2)
    pool = jnp.where(same, 1.0 / 16.0, 0.0)
    rows = x.shape[0]
    means = jnp.dot(
        jnp.concatenate([x, y, x * x, y * y, x * y], axis=0),
        pool,
        precision=HIGHEST,
        preferred_element_type=F32,
    )
    mx, my, exx, eyy, exy = (means[k * rows : (k + 1) * rows] for k in range(5))
    n1 = 2.0 * mx * my + SSIM_MEAN
    n2 = 2.0 * (exy - mx * my) + SSIM_SPREAD
    d1 = mx * mx + my * my + SSIM_MEAN
    d2 = (exx - mx * mx) + (eyy - my * my) + SSIM_SPREAD
    i1, i2 = 1.0 / d1, 1.0 / d2
    both = i1 * i2
    ratio = n1 * n2 * both
    by_mean = 2.0 * my * (n2 - n1) * both + 2.0 * mx * ratio * (i2 - i1)
    by_square = -ratio * i2
    by_cross = 2.0 * n1 * both
    return 0.1 * (x - y) - (0.2 / 16.0) * (by_mean + 2.0 * x * by_square + y * by_cross)


def render_kernel(arr_ref, tgt_ref, img_ref, ret_ref, xq, rq, perm, bc, a_s, w_s, tg, gr, pic, tgt, slope, mono):
    mono[...] = monomials()
    for q in range(QUADS):
        xq[q] = arr_ref[:, q, :]
    sub = iota((8, PIX), 0)

    def shifted(values, by, fill):
        keep = (sub >= by) if by > 0 else (sub < 8 + by)
        return jnp.where(keep, pltpu.roll(values, by % 8, 0), fill)

    def block(q, carry):
        x = xq[q]
        turned = x.T
        keys = jnp.concatenate(
            [turned[c * WIDE + KEY : c * WIDE + KEY + 1, :] for c in range(CAP)], axis=1
        )
        count = jnp.zeros((8, PLACES), F32)
        for c in range(CAP):
            column = x[:, c * WIDE + KEY : c * WIDE + KEY + 1]
            less = jnp.where(column < keys, 1.0, 0.0)
            count = count + jnp.sum(less.reshape(8, 8, PLACES), axis=0)
        rank = jnp.sum(count, axis=0, keepdims=True)
        filled = jnp.sum(jnp.where(keys > 0.0, 1.0, 0.0)).astype(jnp.int32)
        run = ((filled + 15) // 16) * 2
        at = iota((PLACES, 128), 0)
        step = at >> 3
        wanted = (at & 7) * run + step + (PLACES - filled)
        wanted = jnp.where(step < run, wanted, -1).astype(F32)
        for t in range(PLACES // 128):
            here = rank[:, t * 128 : (t + 1) * 128]
            perm[:, t * 128 : (t + 1) * 128] = jnp.where(here == wanted, 1.0, 0.0).astype(BF16)
        parts = three_parts(x)
        lane = iota((GS, 128), 1)
        gathered = []
        for c in range(CAP):
            turn = [pltpu.roll(parts[k], (WIDE * (k - c)) % 128, 1) for k in range(3)]
            gathered.append(
                jnp.where(
                    lane < WIDE,
                    turn[0],
                    jnp.where(lane < 2 * WIDE, turn[1], jnp.where(lane < 3 * WIDE, turn[2], 0.0)),
                )
            )
        payload = jnp.concatenate(gathered, axis=0).astype(BF16)
        ordered = jnp.dot(perm[...], payload, preferred_element_type=F32).astype(BF16)
        bc[...] = jnp.dot(ordered, mono[...], preferred_element_type=F32)

        def ahead(i, carry):
            passing, seen = list(carry[0]), [list(s) for s in carry[1]]
            rows = pl.ds(pl.multiple_of(i * 8, 8), 8)
            power, first, second, opacity, c0, c1, c2 = (
                bc[rows, k * 128 : (k + 1) * 128] for k in range(7)
            )
            for t in range(TILES):
                alpha = opacity * jnp.exp(power)
                weight = passing[t] * alpha
                passing[t] = passing[t] - weight
                a_s[rows, t * 128 : (t + 1) * 128] = alpha
                w_s[rows, t * 128 : (t + 1) * 128] = weight
                for k, colour in enumerate((c0, c1, c2)):
                    seen[k][t] = seen[k][t] + colour * weight
                power = power + first
                first = first + second
            return tuple(passing), tuple(tuple(s) for s in seen)

        one = jnp.ones((8, 128), F32)
        zero = jnp.zeros((8, 128), F32)
        start = ((one,) * TILES, ((zero,) * TILES,) * 3)
        passing, seen = lax.fori_loop(
            0, run // 2, lambda i, s: ahead(2 * i + 1, ahead(2 * i, s)), start
        )
        left = jnp.concatenate(passing, axis=1)
        seen = [jnp.concatenate(s, axis=1) for s in seen]
        before = shifted(left, 1, 1.0)
        for by in (1, 2, 4):
            before = before * shifted(before, by, 1.0)
        for k in range(3):
            image = jnp.sum(before * seen[k], axis=0, keepdims=True)
            img_ref[q, k : k + 1, :] = image
            for t in range(TILES):
                pic[k * 8 + t : k * 8 + t + 1, :] = image[:, t * 128 : (t + 1) * 128]
                tgt[k * 8 + t : k * 8 + t + 1, :] = tgt_ref[q, k : k + 1, t * 128 : (t + 1) * 128]
        slope[...] = loss_slope(pic[...], tgt[...])
        behind = jnp.zeros((8, PIX), F32)
        for k in range(3):
            row = jnp.concatenate([slope[k * 8 + t : k * 8 + t + 1, :] for t in range(TILES)], axis=1)
            behind = behind + row * seen[k]
            tg[k] = before * row
        value, factor = shifted(behind, -1, 0.0), shifted(left, -1, 0.0)
        for by in (1, 2, 4):
            value = value + factor * shifted(value, -by, 0.0)
            factor = factor * shifted(factor, -by, 0.0)
        value = before * value
        gr[...] = jnp.zeros((PLACES, 128), F32)
        lane8 = iota((8, 128), 1)
        across = ((lane8 & 31) - 16).astype(F32)
        down = ((lane8 >> 5) - 16).astype(F32)
        slot = lane8 & 7

        def back(i, later):
            later = list(later)
            rows = pl.ds(pl.multiple_of(i * 8, 8), 8)
            c0, c1, c2 = (bc[rows, k * 128 : (k + 1) * 128] for k in (4, 5, 6))
            plain, graded = zero, zero
            colours = [zero, zero, zero]
            for t in range(TILES - 1, -1, -1):
                cols = slice(t * 128, (t + 1) * 128)
                alpha, weight = a_s[rows, cols], w_s[rows, cols]
                g0, g1, g2 = (tg[k, :, cols] for k in range(3))
                gap = c0 * g0 + c1 * g1 + c2 * g2 - later[t]
                later[t] = later[t] + alpha * gap
                plain = plain + weight * gap
                if t:
                    graded = graded + plain
                colours = [colours[0] + weight * g0, colours[1] + weight * g1, colours[2] + weight * g2]
            sums = colours + [plain * across, plain * down + 4.0 * graded, plain]
            out = zero
            for k, value in enumerate(sums):
                out = jnp.where(slot == k, jnp.sum(value, axis=1, keepdims=True), out)
            gr[rows, :] = out
            return tuple(later)

        lax.fori_loop(
            0,
            run // 2,
            lambda i, s: back(run - 2 - 2 * i, back(run - 1 - 2 * i, s)),
            tuple(value[:, t * 128 : (t + 1) * 128] for t in range(TILES)),
        )
        grads = gr[...]
        high = grads.astype(BF16)
        low = (grads - high.astype(F32)).astype(BF16)
        placed = lax.dot_general(
            perm[...],
            jnp.concatenate([high, low], axis=1),
            (((0,), (0,)), ((), ())),
            preferred_element_type=F32,
        )
        placed = placed[:, 0:128] + placed[:, 128:256]
        group = iota((GS, 128), 1) >> 3
        total = jnp.zeros((GS, 128), F32)
        for c in range(CAP):
            total = jnp.where(group == (q & 1) * 8 + c, placed[c * GS : (c + 1) * GS, :], total)
        rq[q] = total
        return carry

    lax.fori_loop(0, QUADS, block, 0)
    for j in range(QUADS // 2):
        ret_ref[:, j, :] = rq[2 * j] + rq[2 * j + 1]


def unpack_kernel(ret_ref, slot_ref, mean_ref, conic_ref, part_ref, mean_grad_ref):
    slot = slot_ref[...]
    owner = jnp.where(iota((GS, G), 0) == (slot >> 5), 1.0, 0.0).astype(BF16)
    owner = jnp.concatenate([owner] * 3, axis=0)
    place = slot & 31
    total = jnp.zeros((BACK, G), F32)
    for j in range(QUADS // 2):
        parts = jnp.concatenate(three_parts(ret_ref[:, j, :]), axis=0).astype(BF16)
        spread = lax.dot_general(
            parts, owner, (((0,), (0,)), ((), ())), preferred_element_type=F32
        )
        for i in range(16):
            total = jnp.where(place == j * 16 + i, spread[i * BACK : (i + 1) * BACK, :], total)
    m, n = centre(mean_ref[0:1, :]), centre(mean_ref[1:2, :])
    a, b, c = (conic_ref[k : k + 1, :] * (1.0 / 32.0) for k in range(3))
    plain = total[5:6, :]
    du = total[3:4, :] - m * plain
    dw = total[4:5, :] - n * plain
    part_ref[0:3, :] = total[0:3, :]
    part_ref[3:4, :] = plain
    mean_grad_ref[0:1, :] = a * du + b * dw
    mean_grad_ref[1:2, :] = b * du + c * dw


def final_kernel(part_ref, angle_ref, logit_ref, sh_ref, logit_grad_ref):
    plain = part_ref[0, 3:4, :]
    for v in range(1, VIEWS):
        plain = plain + part_ref[v, 3:4, :]
    logit_grad_ref[...] = plain * (1.0 - jax.nn.sigmoid(logit_ref[...]))
    polar = jnp.concatenate([angle_ref[v, 0:1, :] for v in range(VIEWS)], axis=0)
    azimuth = jnp.concatenate([angle_ref[v, 1:2, :] for v in range(VIEWS)], axis=0)
    basis = sh_basis(polar, azimuth)
    for k in range(16):
        total = part_ref[0, 0:3, :] * basis[k][0:1, :]
        for v in range(1, VIEWS):
            total = total + part_ref[v, 0:3, :] * basis[k][v : v + 1, :]
        sh_ref[3 * k : 3 * k + 3, :] = total


VM = pl.BlockSpec(memory_space=pltpu.VMEM)


def call(kernel, ins, outs, scratch=(), limit=48):
    single = not isinstance(outs, list)
    shapes = [outs] if single else outs
    got = pl.pallas_call(
        kernel,
        out_shape=[jax.ShapeDtypeStruct(s, F32) for s in shapes],
        in_specs=[VM] * len(ins),
        out_specs=[VM] * len(shapes),
        scratch_shapes=list(scratch),
        compiler_params=pltpu.CompilerParams(vmem_limit_bytes=limit * 2**20),
    )(*ins)
    return got[0] if single else got


def pack(sh_coef, logit, angle, mean, conic, slot, rank):
    return call(
        pack_kernel,
        [sh_coef, logit, angle, mean, conic, slot, rank],
        (GS, QUADS, 128),
        [pltpu.VMEM((WIDE, G), F32)],
    )


def render(arrived, target):
    return call(
        render_kernel,
        [arrived, target],
        [(QUADS, 3, PIX), (GS, QUADS // 2, 128)],
        [
            pltpu.VMEM((QUADS, GS, 128), F32),
            pltpu.VMEM((QUADS, GS, 128), F32),
            pltpu.VMEM((PLACES, PLACES), BF16),
            pltpu.VMEM((PLACES, 7 * 128), F32),
            pltpu.VMEM((PLACES, PIX), F32),
            pltpu.VMEM((PLACES, PIX), F32),
            pltpu.VMEM((3, 8, PIX), F32),
            pltpu.VMEM((PLACES, 128), F32),
            pltpu.VMEM((24, 128), F32),
            pltpu.VMEM((24, 128), F32),
            pltpu.VMEM((24, 128), F32),
            pltpu.VMEM((128, 7 * 128), BF16),
        ],
    )


def unpack(back, slot, mean, conic):
    return call(unpack_kernel, [back, slot, mean, conic], [(4, G), (2, G)])


def final(parts, angles, logit):
    return call(final_kernel, [parts, angles, logit], [(48, G), (1, G)])


def local(sh_coef, opacity_logit, view_angle, mean_pos, conic, send_slot, depth_rank, target):
    logit = opacity_logit.reshape(1, G)
    sent = pack(sh_coef, logit, view_angle[0], mean_pos[0], conic[0], send_slot, depth_rank)
    arrived = lax.all_to_all(sent, "gs", split_axis=0, concat_axis=0, tiled=True)
    angles = lax.all_gather(view_angle[0], "view")
    images, back = render(arrived, target[0])
    returned = lax.all_to_all(back, "gs", split_axis=0, concat_axis=0, tiled=True)
    part, mean_grad = unpack(returned, send_slot, mean_pos[0], conic[0])
    parts = lax.all_gather(part, "view")
    sh_grad, logit_grad = final(parts, angles, logit)
    return (sh_grad, logit_grad.reshape(G), mean_grad[None], images[None])


def solution(mesh):
    return jax.shard_map(
        local,
        mesh=mesh,
        in_specs=(
            P(None, "gs"),
            P("gs"),
            P("view", None, "gs"),
            P("view", None, "gs"),
            P("view", None, "gs"),
            P("view", "gs"),
            P("view", "gs"),
            P("view", "gs", None, None),
        ),
        out_specs=(P(None, "gs"), P("gs"), P("view", None, "gs"), P("view", "gs", None, None)),
        check_vma=False,
    )
```

time: 229 us -> 83.1 us (0.36)
  the two profiles are of different devices: /device:TPU:1 before, /device:TPU:6 now
where the time goes in v1:
time: 83.1 us; the launch traced here: 82.7 us
  blocking collectives  26 us (31%)
  Pallas kernels  24.3 us (29%)
  starting transfers between devices  19.8 us (24%)
  waiting for transfers between devices  8.82 us (11%)
  local copies, waits for them, and re-layouts  3.02 us (4%)
    pallas_call x4, Pallas kernels, call(): pl.pallas_call(kernel, out_shape=[jax.ShapeDtypeStruct(s, F32) for s in s...  24.3 us
    all_gather x1, blocking collectives, local(): angles = lax.all_gather(view_angle[0], 'view')  14.1 us
    all_to_all x1, starting transfers between devices, local(): lax.all_to_all(sent, 'gs', split_axis=0, concat_axis=0, tiled=True)  12.3 us
    all_gather x1, blocking collectives, local(): parts = lax.all_gather(part, 'view')  11.9 us
    all_to_all x1, waiting for transfers between devices, local(): lax.all_to_all(sent, 'gs', split_axis=0, concat_axis=0, tiled=True)  8.82 us
    all_to_all x1, starting transfers between devices, local(): lax.all_to_all(back, 'gs', split_axis=0, concat_axis=0, tiled=True)  7.54 us
    unnamed x17, local copies, waits for them, and re-layouts  3.02 us
  transfers between devices with their start and end apart: 2, of which 1 were waited for; matrix products, arithmetic and copies ran while one was open for 1% of the time, Pallas kernels for 0%

profile of v1, /device:TPU:6, one launch (start us, length us, event | category | flops | bytes accessed | tf_op | source)
XLA Modules:
  0.0 82.7 jit_solution(10246134247195279304)
XLA Ops:
  0.6 0.0 copy-start.1
  0.6 0.0 copy-start.2
  0.7 0.0 copy-start.4
  0.7 0.0 copy-start.5
  0.7 0.7 copy.20
  1.4 0.0 copy-start.3
  1.4 0.0 copy-done.1
  1.4 0.0 copy-done.2
  1.4 0.0 copy-done.4
  1.4 0.0 copy-done.5
  1.4 0.6 copy-done.3
  2.1 0.0 copy-start
  2.1 0.9 %copy-done = f32[48,1024]{1,0:T(8,128)S(1)} copy-done((f32[48,1024]{1,0:T(8,128)S(1)}, f32[48,1024]{1,0:T(8,128)}, u32[]{:S(2)}) %copy-start) | copy-done | bytes 196632
  3.0 2.0 %shard_map.111 = f32[64,4,128]{2,1,0:T(4,128)} custom-call(f32[48,1024]{1,0:T(8,128)S(1)} %copy-done, f32[1,1024]{1,0:T(1,128)S(1)} %bitcast.20, f32[2,1024]{1,0:T(2,128)S(1)} %bitcast.17, f32[2,1024]{1,0:T(2,128)S(1)} %bitcast.18, f32[3,1024]{1,0:T(4,128)S(1)} %bitcast.14, s32[1,1024]{1,0:T(1,128)S(1)} %copy-done.3, s32[1,1024]{1,0:T(1,128)S(1)} %copy-done.5), custom_call_target="tpu_custom_call" | custom-call | tf_op jit(solution)/shard_map/pallas_call | solution.py:368
  5.0 0.0 copy-start.6
  5.0 12.3 %all-to-all-start = ((f32[64,4,128]{2,1,0:T(4,128)}), f32[64,4,128]{2,1,0:T(4,128)S(1)}, u32[]{:S(2)}, u32[]{:S(2)}) async-start(f32[64,4,128]{2,1,0:T(4,128)} %shard_map.111), calls=%async_computation | async-start | bytes 262144 | tf_op jit(solution)/shard_map/all_to_all | solution.py:421
  17.3 0.0 copy-done.6
  17.4 8.8 %all-to-all-done.arr_ref = f32[64,4,128]{2,1,0:T(4,128)S(1)} async-done(((f32[64,4,128]{2,1,0:T(4,128)}), f32[64,4,128]{2,1,0:T(4,128)S(1)}, u32[]{:S(2)}, u32[]{:S(2)}) %all-to-all-start) | async-done | bytes 131104 | tf_op jit(solution)/shard_map/all_to_all | solution.py:421
  26.2 20.0 %shard_map.112 = (f32[4,3,1024]{2,1,0:T(4,128)S(1)}, f32[64,2,128]{2,1,0:T(2,128)}) custom-call(f32[64,4,128]{2,1,0:T(4,128)S(1)} %all-to-all-done.arr_ref, f32[4,3,1024]{2,1,0:T(4,128)S(1)} %bitcast.13), custom_call_target="tpu_custom_call" | custom-call | tf_op jit(solution)/shard_map/pallas_call | solution.py:368
  46.2 7.5 %all-to-all-start.1 = ((f32[64,2,128]{2,1,0:T(2,128)}), f32[64,2,128]{2,1,0:T(2,128)S(1)}, u32[]{:S(2)}, u32[]{:S(2)}) async-start(f32[64,2,128]{2,1,0:T(2,128)} %get-tuple-element.10), calls=%async_computation.1 | async-start | bytes 131072 | tf_op jit(solution)/shard_map/all_to_all | solution.py:424
  53.7 14.1 %all_gather.11.angle_ref = f32[4,2,1024]{2,1,0:T(2,128)S(1)} all-gather(f32[1,2,1024]{2,1,0:T(2,128)S(1)} %copy-done.1), channel_id=1, replica_groups=mesh['gs'=64,'view'=4] {'view'}, dimensions={0}, use_global_device_ids=true | all-gather | bytes 40960 | tf_op jit(solution)/shard_map/all_gather | solution.py:422
  67.9 0.7 copy.15
  68.5 0.0 all-to-all-done.1.ret_ref
  68.5 1.1 %shard_map.113 = (f32[4,1024]{1,0:T(4,128)S(1)}, f32[2,1024]{1,0:T(2,128)}) custom-call(f32[64,2,128]{2,1,0:T(2,128)S(1)} %all-to-all-done.1.ret_ref, s32[1,1024]{1,0:T(1,128)S(1)} %copy-done.3, f32[2,1024]{1,0:T(2,128)S(1)} %bitcast.19, f32[3,1024]{1,0:T(4,128)S(1)} %bitcast.15), custom_call_target="tpu_custom_call" | custom-call | tf_op jit(solution)/shard_map/pallas_call | solution.py:368
  69.7 11.9 %all-gather.1.part_ref = f32[4,4,1024]{2,1,0:T(4,128)S(1)} all-gather(f32[1,4,1024]{2,1,0:T(4,128)S(1)} %bitcast.22), channel_id=2, replica_groups=mesh['gs'=64,'view'=4] {'view'}, dimensions={0}, use_global_device_ids=true | all-gather | bytes 81920 | tf_op jit(solution)/shard_map/all_gather | solution.py:426
  81.5 1.2 %shard_map.114 = (f32[48,1024]{1,0:T(8,128)}, f32[1,1024]{1,0:T(1,128)}) custom-call(f32[4,4,1024]{2,1,0:T(4,128)S(1)} %all-gather.1.part_ref, f32[4,2,1024]{2,1,0:T(2,128)S(1)} %all_gather.11.angle_ref, f32[1,1024]{1,0:T(1,128)S(1)} %bitcast.21), custom_call_target="tpu_custom_call" | custom-call | tf_op jit(solution)/shard_map/pallas_call | solution.py:368
  (1 shorter events, 0.0 us)
Async XLA Ops:
  0.6 0.8 copy-start.1
  0.6 0.8 copy-start.2
  0.7 0.8 copy-start.4
  0.7 0.8 copy-start.5
  1.4 0.7 copy-start.3
  2.1 0.9 %copy-start = (f32[48,1024]{1,0:T(8,128)S(1)}, f32[48,1024]{1,0:T(8,128)}, u32[]{:S(2)}) copy-start(f32[48,1024]{1,0:T(8,128)} %sh_ref.1) | copy-start | bytes 589828
  5.0 12.3 %copy-start.6 = (f32[1,4,3,1024]{3,1,2,0:T(4,128)S(1)}, f32[1,4,3,1024]{3,1,2,0:T(4,128)}, u32[]{:S(2)}) copy-start(f32[1,4,3,1024]{3,1,2,0:T(4,128)} %param.15) | copy-start | bytes 147460
  5.0 21.2 %all-to-all-start = ((f32[64,4,128]{2,1,0:T(4,128)}), f32[64,4,128]{2,1,0:T(4,128)S(1)}, u32[]{:S(2)}, u32[]{:S(2)}) async-start(f32[64,4,128]{2,1,0:T(4,128)} %shard_map.111), calls=%async_computation | async-start | bytes 262144 | tf_op jit(solution)/shard_map/all_to_all | solution.py:421
  46.2 22.4 %all-to-all-start.1 = ((f32[64,2,128]{2,1,0:T(2,128)}), f32[64,2,128]{2,1,0:T(2,128)S(1)}, u32[]{:S(2)}, u32[]{:S(2)}) async-start(f32[64,2,128]{2,1,0:T(2,128)} %get-tuple-element.10), calls=%async_computation.1 | async-start | bytes 131072 | tf_op jit(solution)/shard_map/all_to_all | solution.py:424

commit v2 on v1

--- a/solution.py
+++ b/solution.py
@@ -84,7 +84,69 @@
     return mean * 32.0 - 16.5
 
 
-def pack_kernel(sh_ref, logit_ref, angle_ref, mean_ref, conic_ref, slot_ref, rank_ref, out_ref, pay):
+def peers():
+    return lax.axis_index("gs"), lax.axis_index("view")
+
+
+def greet():
+    me, view = peers()
+    barrier = pltpu.get_barrier_semaphore()
+
+    def one(d, carry):
+        pl.semaphore_signal(barrier, inc=1, device_id=(lax.rem(me + d, GS), view), device_id_type=MESH)
+        return carry
+
+    lax.fori_loop(1, GS, one, 0)
+    for d in range(1, VIEWS):
+        pl.semaphore_signal(barrier, inc=1, device_id=(me, lax.rem(view + d, VIEWS)), device_id_type=MESH)
+
+
+def greeted():
+    pl.semaphore_wait(pltpu.get_barrier_semaphore(), GS - 1 + VIEWS - 1)
+
+
+def deal(sent, got, send_sem, recv_sem):
+    me, view = peers()
+
+    def one(d, carry):
+        other = lax.rem(me + d, GS)
+        pltpu.make_async_remote_copy(
+            src_ref=sent.at[other],
+            dst_ref=got.at[me],
+            send_sem=send_sem,
+            recv_sem=recv_sem,
+            device_id=(other, view),
+            device_id_type=MESH,
+        ).start()
+        return carry
+
+    lax.fori_loop(1, GS, one, 0)
+
+
+def spread_views(mine, got, send_sem, recv_sem):
+    me, view = peers()
+    for d in range(1, VIEWS):
+        pltpu.make_async_remote_copy(
+            src_ref=mine,
+            dst_ref=got.at[view],
+            send_sem=send_sem,
+            recv_sem=recv_sem,
+            device_id=(me, lax.rem(view + d, VIEWS)),
+            device_id_type=MESH,
+        ).start()
+
+
+def settle(whole, count, sem):
+    part = whole.at[pl.ds(0, count)]
+    pltpu.make_async_copy(part, part, sem).wait()
+
+
+def pack_kernel(
+    sh_ref, logit_ref, angle_ref, mean_ref, conic_ref, slot_ref, rank_ref, arr_ref, angles_ref, out_ref, pay, sems
+):
+    greet()
+    me, view = peers()
+    angles_ref[view] = angle_ref[...]
     basis = sh_basis(angle_ref[0:1, :], angle_ref[1:2, :])
     colour = jnp.full((3, G), 0.5, F32)
     for k in range(16):
@@ -116,6 +178,14 @@
                 owner, spread, (((1,), (1,)), ((), ())), preferred_element_type=F32
             )
         out_ref[:, q, :] = total
+    arr_ref[me] = out_ref[me]
+    greeted()
+    deal(out_ref, arr_ref, sems.at[0], sems.at[1])
+    spread_views(angle_ref, angles_ref, sems.at[2], sems.at[3])
+    settle(arr_ref, GS - 1, sems.at[1])
+    settle(angles_ref, VIEWS - 1, sems.at[3])
+    settle(arr_ref, GS - 1, sems.at[0])
+    settle(angles_ref, VIEWS - 1, sems.at[2])
 
 
 def monomials():
@@ -320,12 +390,18 @@
         ret_ref[:, j, :] = rq[2 * j] + rq[2 * j + 1]
 
 
-def unpack_kernel(ret_ref, slot_ref, mean_ref, conic_ref, part_ref, mean_grad_ref):
+def unpack_kernel(sent_ref, slot_ref, mean_ref, conic_ref, parts_ref, mean_grad_ref, ret_ref, part_ref, sems):
+    greet()
+    me, view = peers()
+    ret_ref[me] = sent_ref[me]
     slot = slot_ref[...]
     owner = jnp.where(iota((GS, G), 0) == (slot >> 5), 1.0, 0.0).astype(BF16)
     owner = jnp.concatenate([owner] * 3, axis=0)
     place = slot & 31
     total = jnp.zeros((BACK, G), F32)
+    greeted()
+    deal(sent_ref, ret_ref, sems.at[0], sems.at[1])
+    settle(ret_ref, GS - 1, sems.at[1])
     for j in range(QUADS // 2):
         parts = jnp.concatenate(three_parts(ret_ref[:, j, :]), axis=0).astype(BF16)
         spread = lax.dot_general(
@@ -340,8 +416,13 @@
     dw = total[4:5, :] - n * plain
     part_ref[0:3, :] = total[0:3, :]
     part_ref[3:4, :] = plain
+    spread_views(part_ref, parts_ref, sems.at[2], sems.at[3])
+    parts_ref[view] = part_ref[...]
     mean_grad_ref[0:1, :] = a * du + b * dw
     mean_grad_ref[1:2, :] = b * du + c * dw
+    settle(parts_ref, VIEWS - 1, sems.at[3])
+    settle(ret_ref, GS - 1, sems.at[0])
+    settle(parts_ref, VIEWS - 1, sems.at[2])
 
 
 def final_kernel(part_ref, angle_ref, logit_ref, sh_ref, logit_grad_ref):
@@ -359,10 +440,12 @@
         sh_ref[3 * k : 3 * k + 3, :] = total
 
 
+MESH = pl.DeviceIdType.MESH
 VM = pl.BlockSpec(memory_space=pltpu.VMEM)
 
 
-def call(kernel, ins, outs, scratch=(), limit=48):
+def call(kernel, ins, outs, scratch=(), limit=48, remote=None):
+    extra = {} if remote is None else dict(collective_id=remote, has_side_effects=True)
     single = not isinstance(outs, list)
     shapes = [outs] if single else outs
     got = pl.pallas_call(
@@ -371,7 +454,7 @@
         in_specs=[VM] * len(ins),
         out_specs=[VM] * len(shapes),
         scratch_shapes=list(scratch),
-        compiler_params=pltpu.CompilerParams(vmem_limit_bytes=limit * 2**20),
+        compiler_params=pltpu.CompilerParams(vmem_limit_bytes=limit * 2**20, **extra),
     )(*ins)
     return got[0] if single else got
 
@@ -380,8 +463,13 @@
     return call(
         pack_kernel,
         [sh_coef, logit, angle, mean, conic, slot, rank],
-        (GS, QUADS, 128),
-        [pltpu.VMEM((WIDE, G), F32)],
+        [(GS, QUADS, 128), (VIEWS, 2, G)],
+        [
+            pltpu.VMEM((GS, QUADS, 128), F32),
+            pltpu.VMEM((WIDE, G), F32),
+            pltpu.SemaphoreType.DMA((4,)),
+        ],
+        remote=0,
     )
 
 
@@ -408,7 +496,17 @@
 
 
 def unpack(back, slot, mean, conic):
-    return call(unpack_kernel, [back, slot, mean, conic], [(4, G), (2, G)])
+    return call(
+        unpack_kernel,
+        [back, slot, mean, conic],
+        [(VIEWS, 4, G), (2, G)],
+        [
+            pltpu.VMEM((GS, QUADS // 2, 128), F32),
+            pltpu.VMEM((4, G), F32),
+            pltpu.SemaphoreType.DMA((4,)),
+        ],
+        remote=1,
+    )
 
 
 def final(parts, angles, logit):
@@ -417,13 +515,9 @@
 
 def local(sh_coef, opacity_logit, view_angle, mean_pos, conic, send_slot, depth_rank, target):
     logit = opacity_logit.reshape(1, G)
-    sent = pack(sh_coef, logit, view_angle[0], mean_pos[0], conic[0], send_slot, depth_rank)
-    arrived = lax.all_to_all(sent, "gs", split_axis=0, concat_axis=0, tiled=True)
-    angles = lax.all_gather(view_angle[0], "view")
+    arrived, angles = pack(sh_coef, logit, view_angle[0], mean_pos[0], conic[0], send_slot, depth_rank)
     images, back = render(arrived, target[0])
-    returned = lax.all_to_all(back, "gs", split_axis=0, concat_axis=0, tiled=True)
-    part, mean_grad = unpack(returned, send_slot, mean_pos[0], conic[0])
-    parts = lax.all_gather(part, "view")
+    parts, mean_grad = unpack(back, send_slot, mean_pos[0], conic[0])
     sh_grad, logit_grad = final(parts, angles, logit)
     return (sh_grad, logit_grad.reshape(G), mean_grad[None], images[None])
 

time: 83.1 us -> 59.7 us (0.72)
  the two profiles are of different devices: /device:TPU:6 before, /device:TPU:1 now
where the time goes in v2:
time: 59.7 us; the launch traced here: 59.5 us
  Pallas kernels  55 us (92%)
  local copies, waits for them, and re-layouts  3.78 us (6%)
  between operations  0.73 us (1%)
    pallas_call x4, Pallas kernels, call(): pl.pallas_call(kernel, out_shape=[jax.ShapeDtypeStruct(s, F32) for s in s...  55 us
    unnamed x16, local copies, waits for them, and re-layouts  3.78 us

profile of v2, /device:TPU:1, one launch (start us, length us, event | category | flops | bytes accessed | tf_op | source)
XLA Modules:
  0.0 59.5 jit_solution(14163091415338016224)
XLA Ops:
  0.6 0.7 %copy.18 = f32[1,3,1024]{2,1,0:T(4,128)S(1)} copy(f32[1,3,1024]{2,0,1:T(1,128)} %param.12) | data formatting | bytes 24576
  1.3 0.0 copy-start.1
  1.3 0.0 copy-start.2
  1.4 0.0 copy-start.3
  1.4 0.0 copy-start.4
  1.4 0.0 copy-start.5
  1.4 0.9 %copy.17 = f32[1,4,3,1024]{3,2,1,0:T(4,128)S(1)} copy(f32[1,4,3,1024]{3,1,2,0:T(4,128)} %param.15) | data formatting | bytes 98304 | tf_op args[7]
  2.3 0.0 copy-done.1
  2.3 0.0 copy-done.2
  2.3 0.0 copy-done.3
  2.3 0.0 copy-done.4
  2.3 0.0 copy-done.5
  2.3 0.0 copy-start
  2.3 0.9 %copy-done = f32[48,1024]{1,0:T(8,128)S(1)} copy-done((f32[48,1024]{1,0:T(8,128)S(1)}, f32[48,1024]{1,0:T(8,128)}, u32[]{:S(2)}) %copy-start) | copy-done | bytes 196632
  3.2 16.7 %shard_map.111 = (f32[64,4,128]{2,1,0:T(4,128)S(1)}, f32[4,2,1024]{2,1,0:T(2,128)S(1)}) custom-call(f32[48,1024]{1,0:T(8,128)S(1)} %copy-done, f32[1,1024]{1,0:T(1,128)S(1)} %bitcast.18, f32[2,1024]{1,0:T(2,128)S(1)} %bitcast.21, f32[2,1024]{1,0:T(2,128)S(1)} %bitcast.16, f32[3,1024]{1,0:T(4,128)S(1)} %bitcast.13, s32[1,1024]{1,0:T(1,128)S(1)} %copy-done.2, ...), custom_call_target="tpu_custom_call" | custom-call | tf_op jit(solution)/shard_map/pallas_call | solution.py:451
  19.9 19.5 %shard_map.112 = (f32[4,3,1024]{2,1,0:T(4,128)S(1)}, f32[64,2,128]{2,1,0:T(2,128)S(1)}) custom-call(f32[64,4,128]{2,1,0:T(4,128)S(1)} %get-tuple-element.12.arr_ref, f32[4,3,1024]{2,1,0:T(4,128)S(1)} %bitcast.12), custom_call_target="tpu_custom_call" | custom-call | tf_op jit(solution)/shard_map/pallas_call | solution.py:451
  39.4 17.6 %shard_map.113 = (f32[4,4,1024]{2,1,0:T(4,128)S(1)}, f32[2,1024]{1,0:T(2,128)S(1)}) custom-call(f32[64,2,128]{2,1,0:T(2,128)S(1)} %get-tuple-element.13.sent_ref, s32[1,1024]{1,0:T(1,128)S(1)} %copy-done.2, f32[2,1024]{1,0:T(2,128)S(1)} %bitcast.17, f32[3,1024]{1,0:T(4,128)S(1)} %bitcast.14), custom_call_target="tpu_custom_call" | custom-call | tf_op jit(solution)/shard_map/pallas_call | solution.py:451
  57.1 0.7 %copy.13 = f32[1,4,3,1024]{3,1,2,0:T(4,128)} copy(f32[1,4,3,1024]{3,2,1,0:T(4,128)S(1)} %bitcast.15) | data formatting | bytes 98304
  57.7 1.2 %shard_map.114 = (f32[48,1024]{1,0:T(8,128)}, f32[1,1024]{1,0:T(1,128)}) custom-call(f32[4,4,1024]{2,1,0:T(4,128)S(1)} %get-tuple-element.14.part_ref, f32[4,2,1024]{2,1,0:T(2,128)S(1)} %get-tuple-element.15.angle_ref, f32[1,1024]{1,0:T(1,128)S(1)} %bitcast.19), custom_call_target="tpu_custom_call" | custom-call | tf_op jit(solution)/shard_map/pallas_call | solution.py:451
  58.9 0.6 %copy.20 = f32[1,2,1024]{2,1,0:T(2,128)} copy(f32[1,2,1024]{2,1,0:T(2,128)S(1)} %bitcast.20) | data formatting | bytes 16384
Async XLA Ops:
  1.3 0.9 %copy-start.1 = (f32[1,2,1024]{2,1,0:T(2,128)S(1)}, f32[1,2,1024]{2,1,0:T(2,128)}, u32[]{:S(2)}) copy-start(f32[1,2,1024]{2,1,0:T(2,128)} %param.11) | copy-start | bytes 24580
  1.3 0.9 %copy-start.2 = (s32[1,1024]{1,0:T(1,128)S(1)}, s32[1,1024]{1,0:T(1,128)}, u32[]{:S(2)}) copy-start(s32[1,1024]{1,0:T(1,128)} %slot_ref.3) | copy-start | bytes 12292
  1.4 0.9 %copy-start.3 = (f32[1024]{0:T(1024)S(1)}, f32[1024]{0:T(1024)}, u32[]{:S(2)}) copy-start(f32[1024]{0:T(1024)} %param.9) | copy-start | bytes 12292
  1.4 0.9 %copy-start.4 = (f32[1,2,1024]{2,1,0:T(2,128)S(1)}, f32[1,2,1024]{2,1,0:T(2,128)}, u32[]{:S(2)}) copy-start(f32[1,2,1024]{2,1,0:T(2,128)} %param.10) | copy-start | bytes 24580
  1.4 0.9 %copy-start.5 = (s32[1,1024]{1,0:T(1,128)S(1)}, s32[1,1024]{1,0:T(1,128)}, u32[]{:S(2)}) copy-start(s32[1,1024]{1,0:T(1,128)} %rank_ref.1) | copy-start | bytes 12292
  2.3 0.9 %copy-start = (f32[48,1024]{1,0:T(8,128)S(1)}, f32[48,1024]{1,0:T(8,128)}, u32[]{:S(2)}) copy-start(f32[48,1024]{1,0:T(8,128)} %sh_ref.1) | copy-start | bytes 589828

commit v3 on v2

v3 whole, which is shorter than its diff:
```python
import jax
import jax.numpy as jnp
from jax import lax
from jax.experimental import pallas as pl
from jax.experimental.pallas import tpu as pltpu
from jax.sharding import PartitionSpec as P

F32 = jnp.float32
BF16 = jnp.bfloat16

SH_ZERO = 0.28209479177387814
SH_ONE = 0.4886025119029199
SH_TWO = (
    1.0925484305920792,
    -1.0925484305920792,
    0.31539156525252005,
    -1.0925484305920792,
    0.5462742152960396,
)
SH_THREE = (
    -0.5900435899266435,
    2.890611442640554,
    -0.4570457994644658,
    0.3731763325901154,
    -0.4570457994644658,
    1.445305721320277,
    -0.5900435899266435,
)
SSIM_MEAN = 0.0001
SSIM_SPREAD = 0.0009

GS = 64
VIEWS = 4
QUADS = 4
CAP = 8
G = 1024
PLACES = GS * CAP
PIX = 1024
TILES = PIX // 128
WIDE = 16
COL, KEY = 6, 9
BACK = 8
OWN = 7
SHIFT = 64.0
LOG2E = 1.4426950408889634
HALF = 8
PASSES = 8 // HALF
UNROLL = 8
FORMS = 2 * PASSES + 4


def iota(shape, axis):
    return lax.broadcasted_iota(jnp.int32, shape, axis)


def sh_basis(polar, azimuth):
    across = jnp.sin(polar)
    x = across * jnp.cos(azimuth)
    y = across * jnp.sin(azimuth)
    z = jnp.cos(polar)
    xx, yy, zz = x * x, y * y, z * z
    return [
        jnp.full_like(x, SH_ZERO),
        -SH_ONE * y,
        SH_ONE * z,
        -SH_ONE * x,
        SH_TWO[0] * x * y,
        SH_TWO[1] * y * z,
        SH_TWO[2] * (2.0 * zz - xx - yy),
        SH_TWO[3] * x * z,
        SH_TWO[4] * (xx - yy),
        SH_THREE[0] * y * (3.0 * xx - yy),
        SH_THREE[1] * x * y * z,
        SH_THREE[2] * y * (4.0 * zz - xx - yy),
        SH_THREE[3] * z * (2.0 * zz - 3.0 * xx - 3.0 * yy),
        SH_THREE[4] * x * (4.0 * zz - xx - yy),
        SH_THREE[5] * z * (xx - yy),
        SH_THREE[6] * x * (xx - 3.0 * yy),
    ]


def three_parts(values):
    high = values.astype(BF16).astype(F32)
    rest = values - high
    middle = rest.astype(BF16).astype(F32)
    return high, middle, rest - middle


def centre(mean):
    return mean * 32.0 - 16.5


def peers():
    return lax.axis_index("gs"), lax.axis_index("view")


def far_first(me):
    across = [((me // 16 + d) % 4) * 16 for d in range(4)]
    along = [((me // 2 + d) % 8) * 2 for d in range(8)]
    core = [me % 2, 1 - me % 2]
    steps = [(x, z, c) for x in range(4) for z in range(8) for c in range(2)]
    steps.sort(key=lambda s: (-min(s[0], 4 - s[0]) - min(s[1], 8 - s[1]), -s[2]))
    return [across[x] + along[z] + core[c] for x, z, c in steps if (x, z, c) != (0, 0, 0)]


def greet():
    me, view = peers()
    barrier = pltpu.get_barrier_semaphore()
    for other in far_first(me):
        pl.semaphore_signal(barrier, inc=1, device_id=(other, view), device_id_type=MESH)
    for d in range(1, VIEWS):
        pl.semaphore_signal(barrier, inc=1, device_id=(me, lax.rem(view + d, VIEWS)), device_id_type=MESH)


def greeted():
    pl.semaphore_wait(pltpu.get_barrier_semaphore(), GS - 1 + VIEWS - 1)


def deal(sent, got, send_sem, recv_sem):
    me, view = peers()
    for other in far_first(me):
        pltpu.make_async_remote_copy(
            src_ref=sent.at[other],
            dst_ref=got.at[me],
            send_sem=send_sem,
            recv_sem=recv_sem,
            device_id=(other, view),
            device_id_type=MESH,
        ).start()


def spread_views(mine, got, send_sem, recv_sem):
    me, view = peers()
    for d in range(1, VIEWS):
        pltpu.make_async_remote_copy(
            src_ref=mine,
            dst_ref=got.at[view],
            send_sem=send_sem,
            recv_sem=recv_sem,
            device_id=(me, lax.rem(view + d, VIEWS)),
            device_id_type=MESH,
        ).start()


def settle(whole, count, sem):
    part = whole.at[pl.ds(0, count)]
    pltpu.make_async_copy(part, part, sem).wait()


def pack_kernel(*refs):
    far, (arr_ref, angles_ref, own_ref, aim_ref), rest = refs[:8], refs[8:12], refs[12:]
    near, (out_ref, pay, sems, load_sems) = rest[:7], rest[7:]
    loads = [
        pltpu.make_async_copy(src, dst, load_sems.at[k])
        for k, (src, dst) in enumerate(zip(far, (*near, aim_ref)))
    ]
    for load in loads:
        load.start()
    greet()
    for load in loads:
        load.wait()
    sh_ref, logit_ref, angle_ref, mean_ref, conic_ref, slot_ref, rank_ref = near
    me, view = peers()
    angles_ref[view] = angle_ref[...]
    basis = sh_basis(angle_ref[0:1, :], angle_ref[1:2, :])
    colour = jnp.full((3, G), 0.5, F32)
    for k in range(16):
        colour = colour + sh_ref[3 * k : 3 * k + 3, :] * basis[k]
    m, n = centre(mean_ref[0:1, :]), centre(mean_ref[1:2, :])
    kept = [slot_ref[...].astype(F32), m, n] + [conic_ref[k] * (1.0 / 32.0) for k in range(3)]
    for k, row in enumerate(kept + [logit_ref[...]]):
        own_ref[k : k + 1, :] = row
    scale = LOG2E / 1024.0
    opacity = 0.99 * jax.nn.sigmoid(logit_ref[...])
    a, b, c = (conic_ref[k] * scale for k in range(3))
    pay[...] = jnp.zeros((WIDE, G), F32)
    away = 0.5 * (a * m * m + 2.0 * b * m * n + c * n * n)
    pay[0:1, :] = (jnp.log(opacity) * LOG2E + SHIFT) - away
    pay[1:2, :] = a * m + b * n
    pay[2:3, :] = b * m + c * n
    pay[3:4, :] = -0.5 * a
    pay[4:5, :] = -b
    pay[5:6, :] = -0.5 * c
    pay[COL : COL + 3, :] = colour
    pay[KEY : KEY + 1, :] = (rank_ref[...] + 1).astype(F32)
    parts = three_parts(pay[...])
    slot = slot_ref[...]
    owner = jnp.where(iota((GS, G), 0) == (slot >> 5), 1.0, 0.0).astype(BF16)
    place = slot & 31
    for q in range(QUADS):
        total = jnp.zeros((GS, 128), F32)
        for part in parts[::-1]:
            spread = jnp.concatenate(
                [jnp.where(place == q * CAP + cap, part, 0.0) for cap in range(CAP)], axis=0
            ).astype(BF16)
            total = total + lax.dot_general(
                owner, spread, (((1,), (1,)), ((), ())), preferred_element_type=F32
            )
        out_ref[:, q, :] = total
    arr_ref[me] = out_ref[me]
    greeted()
    deal(out_ref, arr_ref, sems.at[0], sems.at[1])
    spread_views(angle_ref, angles_ref, sems.at[2], sems.at[3])
    settle(arr_ref, GS - 1, sems.at[1])
    settle(angles_ref, VIEWS - 1, sems.at[3])
    settle(arr_ref, GS - 1, sems.at[0])
    settle(angles_ref, VIEWS - 1, sems.at[2])


def monomials():
    lane = iota((WIDE, 128), 1)
    row = iota((WIDE, 128), 0)
    u = ((lane & 31) - 16).astype(F32)
    top = ((lane >> 5) - 16).astype(F32)

    def rows(entries):
        out = jnp.zeros((WIDE, 128), F32)
        for k, value in entries.items():
            out = jnp.where(row == k, value, out)
        return out

    def power(w):
        return rows({0: 1.0, 1: u, 2: w, 3: u * u, 4: u * w, 5: w * w})

    def first(w):
        return rows({2: 4.0, 4: 4.0 * u, 5: 8.0 * w + 16.0})

    tiles = []
    for h in range(PASSES):
        tiles += [power(top + 4.0 * HALF * h), first(top + 4.0 * HALF * h)]
    tiles.append(rows({5: 32.0}))
    tiles += [rows({COL + c: 1.0}) for c in range(3)]
    base = jnp.concatenate(tiles, axis=1)
    shift = jnp.where(
        (iota((WIDE, 128), 0) == 0) & (iota((WIDE, 128), 1) >= 0), -SHIFT, 0.0
    )
    none = jnp.zeros((WIDE, 128), F32)
    shift = jnp.concatenate([shift, none] * PASSES + [none] * 4, axis=1)
    return jnp.concatenate([base, base, base, shift], axis=0).astype(BF16)


def loss_slope(x, y):
    lane = iota((128, 128), 1)
    other = iota((128, 128), 0)
    same = ((lane & 31) >> 2) == ((other & 31) >> 2)
    pool = jnp.where(same, 1.0 / 16.0, 0.0).astype(BF16)
    rows = x.shape[0]
    parts = three_parts(jnp.concatenate([x, y, x * x, y * y, x * y], axis=0))
    sums = jnp.dot(
        jnp.concatenate(parts, axis=0).astype(BF16), pool, preferred_element_type=F32
    )
    means = (sums[10 * rows : 15 * rows] + sums[5 * rows : 10 * rows]) + sums[0 : 5 * rows]
    mx, my, exx, eyy, exy = (means[k * rows : (k + 1) * rows] for k in range(5))
    n1 = 2.0 * mx * my + SSIM_MEAN
    n2 = 2.0 * (exy - mx * my) + SSIM_SPREAD
    d1 = mx * mx + my * my + SSIM_MEAN
    d2 = (exx - mx * mx) + (eyy - my * my) + SSIM_SPREAD
    i1, i2 = 1.0 / d1, 1.0 / d2
    both = i1 * i2
    ratio = n1 * n2 * both
    by_mean = 2.0 * my * (n2 - n1) * both + 2.0 * mx * ratio * (i2 - i1)
    by_square = -ratio * i2
    by_cross = 2.0 * n1 * both
    return 0.1 * (x - y) - (0.2 / 16.0) * (by_mean + 2.0 * x * by_square + y * by_cross)


def shifted(values, by, fill):
    sub = iota(values.shape, 0)
    keep = (sub >= by) if by > 0 else (sub < 8 + by)
    return jnp.where(keep, pltpu.roll(values, by % 8, 0), fill)


def order(x, perm, bc, mono, step_s, sub_s):
    turned = x.T
    packed = jnp.concatenate([turned[c * WIDE : (c + 1) * WIDE, :] for c in range(CAP)], axis=1)
    parts = jnp.concatenate(three_parts(packed), axis=0).astype(BF16)
    keys = packed[KEY : KEY + 1, :]
    pick = jnp.where((iota((3 * WIDE, 128), 0) & 15) == KEY, 1.0, 0.0).astype(BF16)
    column = lax.dot_general(parts, pick, (((0,), (0,)), ((), ())), preferred_element_type=F32)
    filled = jnp.sum(jnp.where(keys > 0.0, 1.0, 0.0))
    run = ((filled.astype(jnp.int32) + 8 * UNROLL - 1) // (8 * UNROLL)) * UNROLL
    span = run.astype(F32)
    step = step_s[...]
    wanted = jnp.where(step < span, sub_s[...] * span + step + (PLACES - filled), -1.0)
    for t in range(PLACES // 128):
        less = jnp.where(column < keys[:, tile(t)], 1.0, 0.0)
        rank = jnp.sum(less, axis=0, keepdims=True)
        perm[:, tile(t)] = jnp.where(rank == wanted, 1.0, 0.0).astype(BF16)
    ordered = lax.dot_general(
        parts, perm[...], (((1,), (1,)), ((), ())), preferred_element_type=F32
    )
    ordered = jnp.concatenate([ordered, jnp.ones((WIDE, PLACES), F32)], axis=0).astype(BF16)
    bc[...] = lax.dot_general(
        ordered, mono[...], (((0,), (0,)), ((), ())), preferred_element_type=F32
    )
    return run


def unroll_loop(run, body, start):
    def several(i, state):
        for k in range(UNROLL):
            state = body(i * UNROLL + k, state)
        return state

    return lax.fori_loop(0, run // UNROLL, several, start)


def tile(t):
    return slice(t * 128, (t + 1) * 128)


def blend(run, bc, a_s, w_s, left, seen):
    one = jnp.ones((8, 128), F32)
    zero = jnp.zeros((8, 128), F32)
    for h in range(PASSES):

        def ahead(i, state, h=h):
            passing, got = list(state[0]), [list(s) for s in state[1]]
            rows = pl.ds(pl.multiple_of(i * 8, 8), 8)
            power, first = bc[rows, tile(2 * h)], bc[rows, tile(2 * h + 1)]
            second = bc[rows, tile(2 * PASSES)]
            colours = [bc[rows, tile(2 * PASSES + 1 + c)] for c in range(3)]
            for t in range(HALF):
                alpha = jnp.exp2(power)
                weight = passing[t] * alpha
                passing[t] = passing[t] - weight
                a_s[rows, tile(h * HALF + t)] = alpha
                w_s[rows, tile(h * HALF + t)] = weight
                for c in range(3):
                    got[c][t] = got[c][t] + colours[c] * weight
                if t < HALF - 1:
                    power = power + first
                    first = first + second
            return tuple(passing), tuple(tuple(s) for s in got)

        passing, got = unroll_loop(run, ahead, ((one,) * HALF, ((zero,) * HALF,) * 3))
        for t in range(HALF):
            left[:, tile(h * HALF + t)] = passing[t]
            for c in range(3):
                seen[c, :, tile(h * HALF + t)] = got[c][t]


def backward(run, bc, a_s, w_s, tg, later_s, red):
    zero = jnp.zeros((8, 128), F32)
    for h in range(PASSES - 1, -1, -1):

        def back(i, later, h=h):
            later = list(later)
            rows = pl.ds(pl.multiple_of((run - 1 - i) * 8, 8), 8)
            c0, c1, c2 = (bc[rows, tile(2 * PASSES + 1 + c)] for c in range(3))
            plain, graded = zero, zero
            sums = [zero, zero, zero]
            for t in range(HALF - 1, -1, -1):
                cols = tile(h * HALF + t)
                alpha, weight = a_s[rows, cols], w_s[rows, cols]
                g0, g1, g2 = (tg[c, :, cols] for c in range(3))
                gap = c0 * g0 + c1 * g1 + c2 * g2 - later[t]
                later[t] = later[t] + alpha * gap
                plain = plain + weight * gap
                if t:
                    graded = graded + plain
                sums = [sums[0] + weight * g0, sums[1] + weight * g1, sums[2] + weight * g2]
            if h:
                graded = graded + HALF * h * plain
            sums = sums + [plain, graded]
            for k in range(5):
                if h < PASSES - 1:
                    sums[k] = sums[k] + red[rows, tile(k)]
                red[rows, tile(k)] = sums[k]
            return tuple(later)

        unroll_loop(run, back, tuple(later_s[:, tile(h * HALF + t)] for t in range(HALF)))


def join(left, seen, pic, slope, tgt, tg, later, image):
    before = shifted(left[...], 1, 1.0)
    for by in (1, 2, 4):
        before = before * shifted(before, by, 1.0)
    for c in range(3):
        row = jnp.sum(before * seen[c], axis=0, keepdims=True)
        image[c : c + 1, :] = row
        for t in range(TILES):
            pic[c * 8 + t : c * 8 + t + 1, :] = row[:, tile(t)]
    slope[...] = loss_slope(pic[...], tgt[...])
    behind = jnp.zeros((8, PIX), F32)
    for c in range(3):
        row = jnp.concatenate([slope[c * 8 + t : c * 8 + t + 1, :] for t in range(TILES)], axis=1)
        behind = behind + row * seen[c]
        tg[c] = before * row
    value, factor = shifted(behind, -1, 0.0), shifted(left[...], -1, 0.0)
    for by in (1, 2, 4):
        value = value + factor * shifted(value, -by, 0.0)
        factor = factor * shifted(factor, -by, 0.0)
    later[...] = before * value


def render_kernel(
    arr_ref, tgt_ref, img_ref, red, perm, runs,
    bc, a_s, w_s, left, seen, tg, later, pic, tgt, slope, mono, xq, image, step_s, sub_s
):
    mono[...] = monomials()
    at = iota((PLACES, 128), 0)
    step_s[...] = (at >> 3).astype(F32)
    sub_s[...] = (at & 7).astype(F32)
    for q in range(QUADS):
        xq[q] = arr_ref[:, q, :]
        for c in range(3):
            for t in range(TILES):
                tgt[q, c * 8 + t : c * 8 + t + 1, :] = tgt_ref[c, q : q + 1, tile(t)]

    def block(q, carry):
        run = order(xq[q], perm.at[q], bc, mono, step_s, sub_s)
        blend(run, bc, a_s, w_s, left, seen)
        join(left, seen, pic, slope, tgt.at[q], tg, later, image.at[q])
        backward(run, bc, a_s, w_s, tg, later, red.at[q])
        runs[q] = jnp.full((8, 128), 8 * run, jnp.int32).astype(F32)
        return carry

    lax.fori_loop(0, QUADS, block, 0)
    for q in range(QUADS):
        for c in range(3):
            img_ref[c, q : q + 1, :] = image[q, c : c + 1, :]


def send_back(red_ref, perm_ref, runs_ref, sent, back):
    pixel = iota((128, 128), 0)
    across = ((pixel & 31) - 16).astype(F32)
    down = ((pixel >> 5) - 16).astype(F32)
    row = iota((BACK, 128), 1).astype(F32)

    def block(q, carry):
        groups = []
        for n in range(PLACES // 128):
            g0, g1, g2, plain, graded = (red_ref[q, tile(n), tile(k)].T for k in range(5))
            sums = (g0, g1, g2, plain * across, plain * down + 4.0 * graded, plain)
            sums = [jnp.sum(value, axis=0, keepdims=True) for value in sums]
            sums = jnp.concatenate(sums + [jnp.zeros((BACK - 6, 128), F32)], axis=0)
            groups.append(jnp.where(row + n * 128.0 < runs_ref[q], sums, 0.0))
        parts = jnp.concatenate(three_parts(jnp.concatenate(groups, axis=1)), axis=0)
        placed = jnp.dot(parts.astype(BF16), perm_ref[q], preferred_element_type=F32)
        placed = (placed[2 * BACK :] + placed[BACK : 2 * BACK]) + placed[0:BACK]
        rows = [placed[:, c * GS : (c + 1) * GS] for c in range(CAP)]
        back[q] = jnp.concatenate(rows, axis=0).T
        return carry

    lax.fori_loop(0, QUADS, block, 0)
    for j in range(QUADS // 2):
        sent[:, j, :] = jnp.concatenate([back[2 * j], back[2 * j + 1]], axis=1)


def unpack_kernel(
    red_ref, perm_ref, runs_ref, own_ref, angles_ref, parts_ref, mean_grad_ref, basis_ref,
    sent_ref, back, ret_ref, part_ref, sems
):
    greet()
    me, view = peers()
    send_back(red_ref, perm_ref, runs_ref, sent_ref, back)
    ret_ref[me] = sent_ref[me]
    slot = own_ref[0:1, :].astype(jnp.int32)
    owner = jnp.where(iota((GS, G), 0) == (slot >> 5), 1.0, 0.0).astype(BF16)
    owner = jnp.concatenate([owner] * 3, axis=0)
    place = slot & 31
    total = jnp.zeros((BACK, G), F32)
    greeted()
    deal(sent_ref, ret_ref, sems.at[0], sems.at[1])
    polar = jnp.concatenate([angles_ref[v, 0:1, :] for v in range(VIEWS)], axis=0)
    azimuth = jnp.concatenate([angles_ref[v, 1:2, :] for v in range(VIEWS)], axis=0)
    for k, values in enumerate(sh_basis(polar, azimuth)):
        basis_ref[k] = values
    settle(ret_ref, GS - 1, sems.at[1])
    for j in range(QUADS // 2):
        parts = jnp.concatenate(three_parts(ret_ref[:, j, :]), axis=0).astype(BF16)
        spread = lax.dot_general(
            parts, owner, (((0,), (0,)), ((), ())), preferred_element_type=F32
        )
        for i in range(16):
            total = jnp.where(place == j * 16 + i, spread[i * BACK : (i + 1) * BACK, :], total)
    m, n, a, b, c = (own_ref[k : k + 1, :] for k in range(1, 6))
    plain = total[5:6, :]
    du = total[3:4, :] - m * plain
    dw = total[4:5, :] - n * plain
    part_ref[0:3, :] = total[0:3, :]
    part_ref[3:4, :] = plain
    spread_views(part_ref, parts_ref, sems.at[2], sems.at[3])
    parts_ref[view] = part_ref[...]
    mean_grad_ref[0:1, :] = a * du + b * dw
    mean_grad_ref[1:2, :] = b * du + c * dw
    settle(parts_ref, VIEWS - 1, sems.at[3])
    settle(ret_ref, GS - 1, sems.at[0])
    settle(parts_ref, VIEWS - 1, sems.at[2])


def final_kernel(part_ref, basis_ref, own_ref, sh_ref, logit_grad_ref):
    plain = part_ref[0, 3:4, :]
    for v in range(1, VIEWS):
        plain = plain + part_ref[v, 3:4, :]
    logit_grad_ref[...] = plain * (1.0 - jax.nn.sigmoid(own_ref[6:7, :]))
    for k in range(16):
        total = part_ref[0, 0:3, :] * basis_ref[k, 0:1, :]
        for v in range(1, VIEWS):
            total = total + part_ref[v, 0:3, :] * basis_ref[k, v : v + 1, :]
        sh_ref[3 * k : 3 * k + 3, :] = total


MESH = pl.DeviceIdType.MESH
VM = pl.BlockSpec(memory_space=pltpu.VMEM)


def call(kernel, ins, outs, scratch=(), limit=16, remote=None, far=False):
    extra = {} if remote is None else dict(collective_id=remote, has_side_effects=True)
    shapes = [o if isinstance(o, jax.ShapeDtypeStruct) else jax.ShapeDtypeStruct(o, F32) for o in outs]
    return pl.pallas_call(
        kernel,
        out_shape=shapes,
        in_specs=[pl.BlockSpec(memory_space=pltpu.HBM) if far else VM] * len(ins),
        out_specs=[VM] * len(shapes),
        scratch_shapes=list(scratch),
        compiler_params=pltpu.CompilerParams(vmem_limit_bytes=limit * 2**20, **extra),
    )(*ins)


def pack(*ins):
    return call(
        pack_kernel,
        [pltpu.with_memory_space_constraint(i, pltpu.HBM) for i in ins],
        [(GS, QUADS, 128), (VIEWS, 2, G), (OWN, G), (3, QUADS, PIX)],
        [pltpu.VMEM(i.shape, i.dtype) for i in ins[:7]]
        + [
            pltpu.VMEM((GS, QUADS, 128), F32),
            pltpu.VMEM((WIDE, G), F32),
            pltpu.SemaphoreType.DMA((4,)),
            pltpu.SemaphoreType.DMA((len(ins),)),
        ],
        remote=0,
        far=True,
    )


def render(arrived, target):
    return call(
        render_kernel,
        [arrived, target],
        [
            (3, QUADS, PIX),
            (QUADS, PLACES, 5 * 128),
            jax.ShapeDtypeStruct((QUADS, PLACES, PLACES), BF16),
            (QUADS, 8, 128),
        ],
        [
            pltpu.VMEM((PLACES, FORMS * 128), F32),
            pltpu.VMEM((PLACES, PIX), F32),
            pltpu.VMEM((PLACES, PIX), F32),
            pltpu.VMEM((8, PIX), F32),
            pltpu.VMEM((3, 8, PIX), F32),
            pltpu.VMEM((3, 8, PIX), F32),
            pltpu.VMEM((8, PIX), F32),
            pltpu.VMEM((24, 128), F32),
            pltpu.VMEM((QUADS, 24, 128), F32),
            pltpu.VMEM((24, 128), F32),
            pltpu.VMEM((4 * WIDE, FORMS * 128), BF16),
            pltpu.VMEM((QUADS, GS, 128), F32),
            pltpu.VMEM((QUADS, 3, PIX), F32),
            pltpu.VMEM((PLACES, 128), F32),
            pltpu.VMEM((PLACES, 128), F32),
        ],
        limit=24,
    )


def unpack(sums, perm, runs, own, angles):
    return call(
        unpack_kernel,
        [sums, perm, runs, own, angles],
        [(VIEWS, 4, G), (2, G), (16, VIEWS, G)],
        [
            pltpu.VMEM((GS, QUADS // 2, 128), F32),
            pltpu.VMEM((QUADS, GS, GS), F32),
            pltpu.VMEM((GS, QUADS // 2, 128), F32),
            pltpu.VMEM((4, G), F32),
            pltpu.SemaphoreType.DMA((4,)),
        ],
        limit=24,
        remote=1,
    )


def final(parts, basis, own):
    return call(final_kernel, [parts, basis, own], [(48, G), (1, G)])


def local(sh_coef, opacity_logit, view_angle, mean_pos, conic, send_slot, depth_rank, target):
    arrived, angles, own, aim = pack(
        sh_coef,
        opacity_logit.reshape(1, G),
        view_angle[0],
        mean_pos[0],
        jnp.transpose(conic, (1, 0, 2)),
        send_slot,
        depth_rank,
        jnp.transpose(target[0], (1, 0, 2)),
    )
    images, sums, perm, runs = render(arrived, aim)
    parts, mean_grad, basis = unpack(sums, perm, runs, own, angles)
    sh_grad, logit_grad = final(parts, basis, own)
    return (sh_grad, logit_grad.reshape(G), mean_grad[None], jnp.transpose(images, (1, 0, 2))[None])


def solution(mesh):
    return jax.shard_map(
        local,
        mesh=mesh,
        in_specs=(
            P(None, "gs"),
            P("gs"),
            P("view", None, "gs"),
            P("view", None, "gs"),
            P("view", None, "gs"),
            P("view", "gs"),
            P("view", "gs"),
            P("view", "gs", None, None),
        ),
        out_specs=(P(None, "gs"), P("gs"), P("view", None, "gs"), P("view", "gs", None, None)),
        check_vma=False,
    )
```

time: 59.7 us -> 45.5 us (0.76)
  Pallas kernels: 55 us -> 44.1 us
  local copies, waits for them, and re-layouts: 3.78 us -> 0.6 us
    pallas_call x4, Pallas kernels: 55 us -> 44.1 us  [call(): pl.pallas_call(kernel, out_shape=shapes, in_specs=[pl.BlockSpec(memory_sp...]
    unnamed x16 -> x1, local copies, waits for them, and re-layouts: 3.78 us -> 0.6 us
where the time goes in v3:
time: 45.5 us; the launch traced here: 45.4 us
  Pallas kernels  44.1 us (97%)
  between operations  0.65 us (1%)
  local copies, waits for them, and re-layouts  0.6 us (1%)
    pallas_call x4, Pallas kernels, call(): pl.pallas_call(kernel, out_shape=shapes, in_specs=[pl.BlockSpec(memory_sp...  44.1 us

profile of v3, /device:TPU:1, one launch (start us, length us, event | category | flops | bytes accessed | tf_op | source)
XLA Modules:
  0.0 45.4 jit_solution(16851627897090140257)
XLA Ops:
  0.6 16.5 %shard_map.111 = (f32[64,4,128]{2,1,0:T(4,128)S(1)}, f32[4,2,1024]{2,1,0:T(2,128)S(1)}, f32[7,1024]{1,0:T(8,128)S(1)}, f32[3,4,1024]{2,1,0:T(4,128)S(1)}) custom-call(f32[48,1024]{1,0:T(8,128)} %refs_0_.1, f32[1,1024]{1,0:T(1,128)} %bitcast.17, f32[2,1024]{1,0:T(2,128)} %bitcast.15, f32[2,1024]{1,0:T(2,128)} %bitcast.16, f32[3,1,1024]{2,1,0:T(1,128)} %bitcast.14, ...), custom_call_target="tpu_custom_call" | custom-call | tf_op jit(solution)/shard_map/pallas_call | solution.py:512
  17.2 11.8 %shard_map.112 = (f32[3,4,1024]{2,1,0:T(4,128)}, f32[4,512,640]{2,1,0:T(8,128)S(1)}, bf16[4,512,512]{2,1,0:T(8,128)(2,1)S(1)}, f32[4,8,128]{2,1,0:T(8,128)S(1)}) custom-call(f32[64,4,128]{2,1,0:T(4,128)S(1)} %get-tuple-element.17.arr_ref, f32[3,4,1024]{2,1,0:T(4,128)S(1)} %get-tuple-element.18.tgt_ref), custom_call_target="tpu_custom_call" | custom-call | tf_op jit(solution)/shard_map/pallas_call | solution.py:512
  28.9 15.0 %shard_map.113 = (f32[4,4,1024]{2,1,0:T(4,128)S(1)}, f32[2,1024]{1,0:T(2,128)S(1)}, f32[16,4,1024]{2,1,0:T(4,128)S(1)}) custom-call(f32[4,512,640]{2,1,0:T(8,128)S(1)} %get-tuple-element.19.red_ref, bf16[4,512,512]{2,1,0:T(8,128)(2,1)S(1)} %get-tuple-element.20.perm_ref, f32[4,8,128]{2,1,0:T(8,128)S(1)} %get-tuple-element.21.runs_ref, ...), custom_call_target="tpu_custom_call" | custom-call | tf_op jit(solution)/shard_map/pallas_call | solution.py:512
  44.0 0.8 %shard_map.114 = (f32[48,1024]{1,0:T(8,128)}, f32[1,1024]{1,0:T(1,128)}) custom-call(f32[4,4,1024]{2,1,0:T(4,128)S(1)} %get-tuple-element.24.part_ref, f32[16,4,1024]{2,1,0:T(4,128)S(1)} %get-tuple-element.25.basis_ref, f32[7,1024]{1,0:T(8,128)S(1)} %get-tuple-element.22.own_ref), custom_call_target="tpu_custom_call" | custom-call | tf_op jit(solution)/shard_map/pallas_call | solution.py:512
  44.8 0.6 %copy.13 = f32[1,2,1024]{2,1,0:T(2,128)} copy(f32[1,2,1024]{2,1,0:T(2,128)S(1)} %bitcast.12) | data formatting | bytes 16384

commit v4 on v3

--- a/solution.py
+++ b/solution.py
@@ -46,6 +46,7 @@
 HALF = 8
 PASSES = 8 // HALF
 UNROLL = 8
+TOGETHER = 4
 FORMS = 2 * PASSES + 4
 
 
@@ -148,18 +149,18 @@
 
 
 def pack_kernel(*refs):
-    far, (arr_ref, angles_ref, own_ref, aim_ref), rest = refs[:8], refs[8:12], refs[12:]
-    near, (out_ref, pay, sems, load_sems) = rest[:7], rest[7:]
+    far, outs, rest = refs[:8], refs[8:15], refs[15:]
+    arr_ref, angles_ref, own_ref, tgt, mono, step_s, sub_s = outs
+    near, (out_ref, pay, sems, load_sems) = rest[:8], rest[8:]
     loads = [
-        pltpu.make_async_copy(src, dst, load_sems.at[k])
-        for k, (src, dst) in enumerate(zip(far, (*near, aim_ref)))
+        pltpu.make_async_copy(src, dst, load_sems.at[k]) for k, (src, dst) in enumerate(zip(far, near))
     ]
     for load in loads:
         load.start()
     greet()
     for load in loads:
         load.wait()
-    sh_ref, logit_ref, angle_ref, mean_ref, conic_ref, slot_ref, rank_ref = near
+    sh_ref, logit_ref, angle_ref, mean_ref, conic_ref, slot_ref, rank_ref, tgt_ref = near
     me, view = peers()
     angles_ref[view] = angle_ref[...]
     basis = sh_basis(angle_ref[0:1, :], angle_ref[1:2, :])
@@ -198,6 +199,14 @@
             )
         out_ref[:, q, :] = total
     arr_ref[me] = out_ref[me]
+    mono[...] = monomials()
+    at = iota((PLACES, 128), 0)
+    step_s[...] = (at >> 3).astype(F32)
+    sub_s[...] = (at & 7).astype(F32)
+    for q in range(QUADS):
+        for c in range(3):
+            for t in range(TILES):
+                tgt[q, c * 8 + t : c * 8 + t + 1, :] = tgt_ref[c, q : q + 1, tile(t)]
     greeted()
     deal(out_ref, arr_ref, sems.at[0], sems.at[1])
     spread_views(angle_ref, angles_ref, sems.at[2], sems.at[3])
@@ -270,30 +279,36 @@
     return jnp.where(keep, pltpu.roll(values, by % 8, 0), fill)
 
 
-def order(x, perm, bc, mono, step_s, sub_s):
-    turned = x.T
-    packed = jnp.concatenate([turned[c * WIDE : (c + 1) * WIDE, :] for c in range(CAP)], axis=1)
-    parts = jnp.concatenate(three_parts(packed), axis=0).astype(BF16)
-    keys = packed[KEY : KEY + 1, :]
+def order(blocks, xs, perm, bc, mono, step_s, sub_s):
     pick = jnp.where((iota((3 * WIDE, 128), 0) & 15) == KEY, 1.0, 0.0).astype(BF16)
-    column = lax.dot_general(parts, pick, (((0,), (0,)), ((), ())), preferred_element_type=F32)
-    filled = jnp.sum(jnp.where(keys > 0.0, 1.0, 0.0))
-    run = ((filled.astype(jnp.int32) + 8 * UNROLL - 1) // (8 * UNROLL)) * UNROLL
-    span = run.astype(F32)
-    step = step_s[...]
-    wanted = jnp.where(step < span, sub_s[...] * span + step + (PLACES - filled), -1.0)
-    for t in range(PLACES // 128):
-        less = jnp.where(column < keys[:, tile(t)], 1.0, 0.0)
-        rank = jnp.sum(less, axis=0, keepdims=True)
-        perm[:, tile(t)] = jnp.where(rank == wanted, 1.0, 0.0).astype(BF16)
-    ordered = lax.dot_general(
-        parts, perm[...], (((1,), (1,)), ((), ())), preferred_element_type=F32
-    )
-    ordered = jnp.concatenate([ordered, jnp.ones((WIDE, PLACES), F32)], axis=0).astype(BF16)
-    bc[...] = lax.dot_general(
-        ordered, mono[...], (((0,), (0,)), ((), ())), preferred_element_type=F32
-    )
-    return run
+    turned = [x.T for x in xs]
+    packed = [
+        jnp.concatenate([t[c * WIDE : (c + 1) * WIDE, :] for c in range(CAP)], axis=1) for t in turned
+    ]
+    parts = [jnp.concatenate(three_parts(p), axis=0).astype(BF16) for p in packed]
+    keys = [p[KEY : KEY + 1, :] for p in packed]
+    columns = [
+        lax.dot_general(p, pick, (((0,), (0,)), ((), ())), preferred_element_type=F32) for p in parts
+    ]
+    filled = [jnp.sum(jnp.where(k > 0.0, 1.0, 0.0), axis=1, keepdims=True) for k in keys]
+    turns = [jnp.floor((f + (8 * UNROLL - 1.0)) * (1.0 / (8 * UNROLL))) for f in filled]
+    step, sub = step_s[...], sub_s[...]
+    for q, key, column, turn, full in zip(blocks, keys, columns, turns, filled):
+        span = turn * UNROLL
+        wanted = jnp.where(step < span, sub * span + step + (PLACES - full), -1.0)
+        for t in range(PLACES // 128):
+            less = jnp.where(column < key[:, tile(t)], 1.0, 0.0)
+            rank = jnp.sum(less, axis=0, keepdims=True)
+            perm[q, :, tile(t)] = jnp.where(rank == wanted, 1.0, 0.0).astype(BF16)
+    ordered = [
+        lax.dot_general(p, perm[q], (((1,), (1,)), ((), ())), preferred_element_type=F32)
+        for q, p in zip(blocks, parts)
+    ]
+    ones = jnp.ones((WIDE, PLACES), F32)
+    ordered = [jnp.concatenate([o, ones], axis=0).astype(BF16) for o in ordered]
+    for q, o in zip(blocks, ordered):
+        bc[q] = lax.dot_general(o, mono[...], (((0,), (0,)), ((), ())), preferred_element_type=F32)
+    return turns
 
 
 def unroll_loop(run, body, start):
@@ -395,28 +410,36 @@
 
 
 def render_kernel(
-    arr_ref, tgt_ref, img_ref, red, perm, runs,
-    bc, a_s, w_s, left, seen, tg, later, pic, tgt, slope, mono, xq, image, step_s, sub_s
+    arr_ref, tgt, mono, step_s, sub_s, img_ref, red, perm, runs,
+    bc, a_s, w_s, left, seen, tg, later, pic, slope, xq, image, runs_s
 ):
-    mono[...] = monomials()
-    at = iota((PLACES, 128), 0)
-    step_s[...] = (at >> 3).astype(F32)
-    sub_s[...] = (at & 7).astype(F32)
     for q in range(QUADS):
         xq[q] = arr_ref[:, q, :]
-        for c in range(3):
-            for t in range(TILES):
-                tgt[q, c * 8 + t : c * 8 + t + 1, :] = tgt_ref[c, q : q + 1, tile(t)]
-
-    def block(q, carry):
-        run = order(xq[q], perm.at[q], bc, mono, step_s, sub_s)
-        blend(run, bc, a_s, w_s, left, seen)
-        join(left, seen, pic, slope, tgt.at[q], tg, later, image.at[q])
-        backward(run, bc, a_s, w_s, tg, later, red.at[q])
-        runs[q] = jnp.full((8, 128), 8 * run, jnp.int32).astype(F32)
+
+    def sort(p, carry):
+        blocks = [p * TOGETHER + k for k in range(TOGETHER)]
+        found = order(blocks, [xq[q] for q in blocks], perm, bc, mono, step_s, sub_s)
+        for q, turn in zip(blocks, found):
+            runs[q] = jnp.broadcast_to(turn * (8 * UNROLL), (8, 128))
+            runs_s[q] = jnp.sum(turn).astype(jnp.int32) * UNROLL
         return carry
 
-    lax.fori_loop(0, QUADS, block, 0)
+    def first(q, carry):
+        blend(runs_s[q], bc.at[q], a_s.at[q], w_s.at[q], left.at[q], seen.at[q])
+        return carry
+
+    def second(q, carry):
+        backward(runs_s[q], bc.at[q], a_s.at[q], w_s.at[q], tg.at[q], later.at[q], red.at[q])
+        return carry
+
+    if TOGETHER == QUADS:
+        sort(0, 0)
+    else:
+        lax.fori_loop(0, QUADS // TOGETHER, sort, 0)
+    lax.fori_loop(0, QUADS, first, 0)
+    for q in range(QUADS):
+        join(left.at[q], seen.at[q], pic.at[q], slope.at[q], tgt.at[q], tg.at[q], later.at[q], image.at[q])
+    lax.fori_loop(0, QUADS, second, 0)
     for q in range(QUADS):
         for c in range(3):
             img_ref[c, q : q + 1, :] = image[q, c : c + 1, :]
@@ -449,7 +472,7 @@
 
 
 def unpack_kernel(
-    red_ref, perm_ref, runs_ref, own_ref, angles_ref, parts_ref, mean_grad_ref, basis_ref,
+    red_ref, perm_ref, runs_ref, own_ref, angles_ref, parts_ref, move_ref, basis_ref,
     sent_ref, back, ret_ref, part_ref, sems
 ):
     greet()
@@ -483,14 +506,15 @@
     part_ref[3:4, :] = plain
     spread_views(part_ref, parts_ref, sems.at[2], sems.at[3])
     parts_ref[view] = part_ref[...]
-    mean_grad_ref[0:1, :] = a * du + b * dw
-    mean_grad_ref[1:2, :] = b * du + c * dw
+    move_ref[0:1, :] = a * du + b * dw
+    move_ref[1:2, :] = b * du + c * dw
     settle(parts_ref, VIEWS - 1, sems.at[3])
     settle(ret_ref, GS - 1, sems.at[0])
     settle(parts_ref, VIEWS - 1, sems.at[2])
 
 
-def final_kernel(part_ref, basis_ref, own_ref, sh_ref, logit_grad_ref):
+def final_kernel(part_ref, move_ref, basis_ref, own_ref, sh_ref, logit_grad_ref, mean_grad_ref):
+    mean_grad_ref[...] = move_ref[...]
     plain = part_ref[0, 3:4, :]
     for v in range(1, VIEWS):
         plain = plain + part_ref[v, 3:4, :]
@@ -506,7 +530,7 @@
 VM = pl.BlockSpec(memory_space=pltpu.VMEM)
 
 
-def call(kernel, ins, outs, scratch=(), limit=16, remote=None, far=False):
+def call(kernel, ins, outs, scratch=(), limit=20, remote=None, far=False):
     extra = {} if remote is None else dict(collective_id=remote, has_side_effects=True)
     shapes = [o if isinstance(o, jax.ShapeDtypeStruct) else jax.ShapeDtypeStruct(o, F32) for o in outs]
     return pl.pallas_call(
@@ -523,8 +547,16 @@
     return call(
         pack_kernel,
         [pltpu.with_memory_space_constraint(i, pltpu.HBM) for i in ins],
-        [(GS, QUADS, 128), (VIEWS, 2, G), (OWN, G), (3, QUADS, PIX)],
-        [pltpu.VMEM(i.shape, i.dtype) for i in ins[:7]]
+        [
+            (GS, QUADS, 128),
+            (VIEWS, 2, G),
+            (OWN, G),
+            (QUADS, 24, 128),
+            jax.ShapeDtypeStruct((4 * WIDE, FORMS * 128), BF16),
+            (PLACES, 128),
+            (PLACES, 128),
+        ],
+        [pltpu.VMEM(i.shape, i.dtype) for i in ins]
         + [
             pltpu.VMEM((GS, QUADS, 128), F32),
             pltpu.VMEM((WIDE, G), F32),
@@ -536,10 +568,10 @@
     )
 
 
-def render(arrived, target):
+def render(*ins):
     return call(
         render_kernel,
-        [arrived, target],
+        ins,
         [
             (3, QUADS, PIX),
             (QUADS, PLACES, 5 * 128),
@@ -547,23 +579,20 @@
             (QUADS, 8, 128),
         ],
         [
-            pltpu.VMEM((PLACES, FORMS * 128), F32),
-            pltpu.VMEM((PLACES, PIX), F32),
-            pltpu.VMEM((PLACES, PIX), F32),
-            pltpu.VMEM((8, PIX), F32),
-            pltpu.VMEM((3, 8, PIX), F32),
-            pltpu.VMEM((3, 8, PIX), F32),
-            pltpu.VMEM((8, PIX), F32),
-            pltpu.VMEM((24, 128), F32),
+            pltpu.VMEM((QUADS, PLACES, FORMS * 128), F32),
+            pltpu.VMEM((QUADS, PLACES, PIX), F32),
+            pltpu.VMEM((QUADS, PLACES, PIX), F32),
+            pltpu.VMEM((QUADS, 8, PIX), F32),
+            pltpu.VMEM((QUADS, 3, 8, PIX), F32),
+            pltpu.VMEM((QUADS, 3, 8, PIX), F32),
+            pltpu.VMEM((QUADS, 8, PIX), F32),
             pltpu.VMEM((QUADS, 24, 128), F32),
-            pltpu.VMEM((24, 128), F32),
-            pltpu.VMEM((4 * WIDE, FORMS * 128), BF16),
+            pltpu.VMEM((QUADS, 24, 128), F32),
             pltpu.VMEM((QUADS, GS, 128), F32),
             pltpu.VMEM((QUADS, 3, PIX), F32),
-            pltpu.VMEM((PLACES, 128), F32),
-            pltpu.VMEM((PLACES, 128), F32),
+            pltpu.SMEM((QUADS,), jnp.int32),
         ],
-        limit=24,
+        limit=44,
     )
 
 
@@ -584,12 +613,12 @@
     )
 
 
-def final(parts, basis, own):
-    return call(final_kernel, [parts, basis, own], [(48, G), (1, G)])
+def final(*ins):
+    return call(final_kernel, ins, [(48, G), (1, G), (2, G)])
 
 
 def local(sh_coef, opacity_logit, view_angle, mean_pos, conic, send_slot, depth_rank, target):
-    arrived, angles, own, aim = pack(
+    arrived, angles, own, *prepared = pack(
         sh_coef,
         opacity_logit.reshape(1, G),
         view_angle[0],
@@ -599,9 +628,9 @@
         depth_rank,
         jnp.transpose(target[0], (1, 0, 2)),
     )
-    images, sums, perm, runs = render(arrived, aim)
-    parts, mean_grad, basis = unpack(sums, perm, runs, own, angles)
-    sh_grad, logit_grad = final(parts, basis, own)
+    images, sums, perm, runs = render(arrived, *prepared)
+    parts, move, basis = unpack(sums, perm, runs, own, angles)
+    sh_grad, logit_grad, mean_grad = final(parts, move, basis, own)
     return (sh_grad, logit_grad.reshape(G), mean_grad[None], jnp.transpose(images, (1, 0, 2))[None])
 
 

time: 45.5 us -> 42.1 us (0.925)
  Pallas kernels: 44.1 us -> 41.4 us
  local copies, waits for them, and re-layouts: 0.6 us -> 0 us
    pallas_call x4, Pallas kernels: 44.1 us -> 41.4 us  [call(): pl.pallas_call(kernel, out_shape=shapes, in_specs=[pl.BlockSpec(memory_sp...]
    unnamed x1 -> x0, local copies, waits for them, and re-layouts: 0.6 us -> none
where the time goes in v4:
time: 42.1 us; the launch traced here: 42 us
  Pallas kernels  41.4 us (98%)
  between operations  0.65 us (2%)
    pallas_call x4, Pallas kernels, call(): pl.pallas_call(kernel, out_shape=shapes, in_specs=[pl.BlockSpec(memory_sp...  41.4 us

profile of v4, /device:TPU:1, one launch (start us, length us, event | category | flops | bytes accessed | tf_op | source)
XLA Modules:
  0.0 42.0 jit_solution(3818691393639540185)
XLA Ops:
  0.6 16.5 %shard_map.111 = (f32[64,4,128]{2,1,0:T(4,128)S(1)}, f32[4,2,1024]{2,1,0:T(2,128)S(1)}, f32[7,1024]{1,0:T(8,128)S(1)}, f32[4,24,128]{2,1,0:T(8,128)S(1)}, bf16[6...) custom-call(f32[48,1024]{1,0:T(8,128)} %refs_0_.1, f32[1,1024]{1,0:T(1,128)} %bitcast.16, ...), custom_call_target="tpu_custom_call" | custom-call | tf_op jit(solution)/shard_map/pallas_call | solution.py:536
  17.2 9.3 %shard_map.112 = (f32[3,4,1024]{2,1,0:T(4,128)}, f32[4,512,640]{2,1,0:T(8,128)S(1)}, bf16[4,512,512]{2,1,0:T(8,128)(2,1)S(1)}, f32[4,8,128]{2,1,0:T(8,128)S(1)}) custom-call(f32[64,4,128]{2,1,0:T(4,128)S(1)} %get-tuple-element.21.arr_ref, f32[4,24,128]{2,1,0:T(8,128)S(1)} %get-tuple-element.22.tgt, bf16[64,768]{1,0:T(8,128)(2,1)S(1)} %get-tuple-element.23.mono, ...), custom_call_target="tpu_custom_call" | custom-call | tf_op jit(solution)/shard_map/pallas_call | solution.py:536
  26.5 14.7 %shard_map.113 = (f32[4,4,1024]{2,1,0:T(4,128)S(1)}, f32[2,1024]{1,0:T(2,128)S(1)}, f32[16,4,1024]{2,1,0:T(4,128)S(1)}) custom-call(f32[4,512,640]{2,1,0:T(8,128)S(1)} %get-tuple-element.26.red_ref, bf16[4,512,512]{2,1,0:T(8,128)(2,1)S(1)} %get-tuple-element.27.perm_ref, f32[4,8,128]{2,1,0:T(8,128)S(1)} %get-tuple-element.28.runs_ref, ...), custom_call_target="tpu_custom_call" | custom-call | tf_op jit(solution)/shard_map/pallas_call | solution.py:536
  41.2 0.8 %shard_map.114 = (f32[48,1024]{1,0:T(8,128)}, f32[1,1024]{1,0:T(1,128)}, f32[2,1024]{1,0:T(2,128)}) custom-call(f32[4,4,1024]{2,1,0:T(4,128)S(1)} %get-tuple-element.31.part_ref, f32[2,1024]{1,0:T(2,128)S(1)} %get-tuple-element.32.move_ref, f32[16,4,1024]{2,1,0:T(4,128)S(1)} %get-tuple-element.33.basis_ref, f32[7,1024]{1,0:T(8,128)S(1)} %get-tuple-element.29.own_ref), custom_call_target="tpu_custom_call" | custom-call | tf_op jit(solution)/shard_map/pallas_call | solution.py:536

commit v5 on v4

--- a/solution.py
+++ b/solution.py
@@ -46,7 +46,8 @@
 HALF = 8
 PASSES = 8 // HALF
 UNROLL = 8
-TOGETHER = 4
+RENDER_MIB = 36
+UNPACK_MIB = 24
 FORMS = 2 * PASSES + 4
 
 
@@ -155,9 +156,9 @@
     loads = [
         pltpu.make_async_copy(src, dst, load_sems.at[k]) for k, (src, dst) in enumerate(zip(far, near))
     ]
+    greet()
     for load in loads:
         load.start()
-    greet()
     for load in loads:
         load.wait()
     sh_ref, logit_ref, angle_ref, mean_ref, conic_ref, slot_ref, rank_ref, tgt_ref = near
@@ -324,7 +325,7 @@
     return slice(t * 128, (t + 1) * 128)
 
 
-def blend(run, bc, a_s, w_s, left, seen):
+def blend(run, bc, a_s, w_s, col, left, seen):
     one = jnp.ones((8, 128), F32)
     zero = jnp.zeros((8, 128), F32)
     for h in range(PASSES):
@@ -335,6 +336,9 @@
             power, first = bc[rows, tile(2 * h)], bc[rows, tile(2 * h + 1)]
             second = bc[rows, tile(2 * PASSES)]
             colours = [bc[rows, tile(2 * PASSES + 1 + c)] for c in range(3)]
+            if h == 0 and col is not None:
+                for c in range(3):
+                    col[rows, tile(c)] = colours[c]
             for t in range(HALF):
                 alpha = jnp.exp2(power)
                 weight = passing[t] * alpha
@@ -355,36 +359,48 @@
                 seen[c, :, tile(h * HALF + t)] = got[c][t]
 
 
-def backward(run, bc, a_s, w_s, tg, later_s, red):
+def back_step(i, later, a_s, w_s, col, tg, red):
     zero = jnp.zeros((8, 128), F32)
-    for h in range(PASSES - 1, -1, -1):
-
-        def back(i, later, h=h):
-            later = list(later)
-            rows = pl.ds(pl.multiple_of((run - 1 - i) * 8, 8), 8)
-            c0, c1, c2 = (bc[rows, tile(2 * PASSES + 1 + c)] for c in range(3))
-            plain, graded = zero, zero
-            sums = [zero, zero, zero]
-            for t in range(HALF - 1, -1, -1):
-                cols = tile(h * HALF + t)
-                alpha, weight = a_s[rows, cols], w_s[rows, cols]
-                g0, g1, g2 = (tg[c, :, cols] for c in range(3))
-                gap = c0 * g0 + c1 * g1 + c2 * g2 - later[t]
-                later[t] = later[t] + alpha * gap
-                plain = plain + weight * gap
-                if t:
-                    graded = graded + plain
-                sums = [sums[0] + weight * g0, sums[1] + weight * g1, sums[2] + weight * g2]
-            if h:
-                graded = graded + HALF * h * plain
-            sums = sums + [plain, graded]
-            for k in range(5):
-                if h < PASSES - 1:
-                    sums[k] = sums[k] + red[rows, tile(k)]
-                red[rows, tile(k)] = sums[k]
-            return tuple(later)
-
-        unroll_loop(run, back, tuple(later_s[:, tile(h * HALF + t)] for t in range(HALF)))
+    later = list(later)
+    rows = pl.ds(pl.multiple_of(i * 8, 8), 8)
+    c0, c1, c2 = (col[rows, tile(c)] for c in range(3))
+    plain, graded = zero, zero
+    sums = [zero, zero, zero]
+    for t in range(TILES - 1, -1, -1):
+        alpha, weight = a_s[rows, tile(t)], w_s[rows, tile(t)]
+        g0, g1, g2 = (tg[c, :, tile(t)] for c in range(3))
+        gap = c0 * g0 + c1 * g1 + c2 * g2 - later[t]
+        later[t] = later[t] + alpha * gap
+        plain = plain + weight * gap
+        if t:
+            graded = graded + plain
+        sums = [sums[0] + weight * g0, sums[1] + weight * g1, sums[2] + weight * g2]
+    for k, value in enumerate(sums + [plain, graded]):
+        red[rows, tile(k)] = value
+    return tuple(later)
+
+
+def backward(run, a_s, w_s, col, tg, later, red):
+    def back(i, state):
+        return back_step(run - 1 - i, state, a_s, w_s, col, tg, red)
+
+    unroll_loop(run, back, tuple(later[:, tile(t)] for t in range(TILES)))
+
+
+def backward_whole(runs, a_s, w_s, col, tg, later, red):
+    steps = PLACES // 8
+    begin = tuple(later[:, tile(t)] for t in range(TILES))
+    last = runs[...] * (1.0 / 8.0) - 1.0
+
+    def several(n, state):
+        for k in range(8):
+            i = steps - 1 - (n * 8 + k)
+            here = last == i.astype(F32)
+            state = [jnp.where(here, b, v) for b, v in zip(begin, state)]
+            state = back_step(i, state, a_s, w_s, col, tg, red)
+        return tuple(state)
+
+    lax.fori_loop(0, steps // 8, several, begin)
 
 
 def join(left, seen, pic, slope, tgt, tg, later, image):
@@ -410,80 +426,96 @@
 
 
 def render_kernel(
-    arr_ref, tgt, mono, step_s, sub_s, img_ref, red, perm, runs,
-    bc, a_s, w_s, left, seen, tg, later, pic, slope, xq, image, runs_s
+    arr_ref, tgt, mono, step_s, sub_s,
+    img_ref, red, perm, runs, largest, a_last, w_last, col_last, tg_last, later_last,
+    bc, a_s, w_s, tg, later, left, seen, pic, slope, xq, image, runs_s
 ):
     for q in range(QUADS):
         xq[q] = arr_ref[:, q, :]
-
-    def sort(p, carry):
-        blocks = [p * TOGETHER + k for k in range(TOGETHER)]
-        found = order(blocks, [xq[q] for q in blocks], perm, bc, mono, step_s, sub_s)
-        for q, turn in zip(blocks, found):
-            runs[q] = jnp.broadcast_to(turn * (8 * UNROLL), (8, 128))
-            runs_s[q] = jnp.sum(turn).astype(jnp.int32) * UNROLL
+    found = order(list(range(QUADS)), [xq[q] for q in range(QUADS)], perm, bc, mono, step_s, sub_s)
+    for q, turn in enumerate(found):
+        runs_s[q] = jnp.sum(turn).astype(jnp.int32) * UNROLL
+    best = jnp.int32(0)
+    for q in range(1, QUADS):
+        best = jnp.where(runs_s[q] > runs_s[best], q, best)
+    last = QUADS - 1
+    largest[...] = jnp.full((8, 128), best, jnp.int32).astype(F32)
+
+    def block(at):
+        return jnp.where(at == best, last, jnp.where(at == last, best, at))
+
+    def first(at, carry):
+        q = block(at)
+        blend(runs_s[q], bc.at[q], a_s.at[at], w_s.at[at], None, left.at[at], seen.at[at])
         return carry
 
-    def first(q, carry):
-        blend(runs_s[q], bc.at[q], a_s.at[q], w_s.at[q], left.at[q], seen.at[q])
+    def second(at, carry):
+        q = block(at)
+        col = bc.at[q, :, pl.ds((2 * PASSES + 1) * 128, 3 * 128)]
+        backward(runs_s[q], a_s.at[at], w_s.at[at], col, tg.at[at], later.at[at], red.at[at])
         return carry
 
-    def second(q, carry):
-        backward(runs_s[q], bc.at[q], a_s.at[q], w_s.at[q], tg.at[q], later.at[q], red.at[q])
-        return carry
-
-    if TOGETHER == QUADS:
-        sort(0, 0)
-    else:
-        lax.fori_loop(0, QUADS // TOGETHER, sort, 0)
-    lax.fori_loop(0, QUADS, first, 0)
-    for q in range(QUADS):
-        join(left.at[q], seen.at[q], pic.at[q], slope.at[q], tgt.at[q], tg.at[q], later.at[q], image.at[q])
-    lax.fori_loop(0, QUADS, second, 0)
+    lax.fori_loop(0, last, first, 0)
+    blend(runs_s[best], bc.at[best], a_last, w_last, col_last, left.at[last], seen.at[last])
+    for at in range(QUADS):
+        q = block(at)
+        runs[at] = jnp.full((8, 128), 8 * runs_s[q], jnp.int32).astype(F32)
+        to = (tg_last, later_last) if at == last else (tg.at[at], later.at[at])
+        join(left.at[at], seen.at[at], pic.at[at], slope.at[at], tgt.at[q], *to, image.at[q])
+    lax.fori_loop(0, last, second, 0)
     for q in range(QUADS):
         for c in range(3):
             img_ref[c, q : q + 1, :] = image[q, c : c + 1, :]
 
 
-def send_back(red_ref, perm_ref, runs_ref, sent, back):
+def reduced(red, runs):
     pixel = iota((128, 128), 0)
     across = ((pixel & 31) - 16).astype(F32)
     down = ((pixel >> 5) - 16).astype(F32)
     row = iota((BACK, 128), 1).astype(F32)
-
-    def block(q, carry):
-        groups = []
-        for n in range(PLACES // 128):
-            g0, g1, g2, plain, graded = (red_ref[q, tile(n), tile(k)].T for k in range(5))
-            sums = (g0, g1, g2, plain * across, plain * down + 4.0 * graded, plain)
-            sums = [jnp.sum(value, axis=0, keepdims=True) for value in sums]
-            sums = jnp.concatenate(sums + [jnp.zeros((BACK - 6, 128), F32)], axis=0)
-            groups.append(jnp.where(row + n * 128.0 < runs_ref[q], sums, 0.0))
-        parts = jnp.concatenate(three_parts(jnp.concatenate(groups, axis=1)), axis=0)
-        placed = jnp.dot(parts.astype(BF16), perm_ref[q], preferred_element_type=F32)
-        placed = (placed[2 * BACK :] + placed[BACK : 2 * BACK]) + placed[0:BACK]
-        rows = [placed[:, c * GS : (c + 1) * GS] for c in range(CAP)]
-        back[q] = jnp.concatenate(rows, axis=0).T
-        return carry
-
-    lax.fori_loop(0, QUADS, block, 0)
+    groups = []
+    for n in range(PLACES // 128):
+        g0, g1, g2, plain, graded = (red[tile(n), tile(k)].T for k in range(5))
+        sums = (g0, g1, g2, plain * across, plain * down + 4.0 * graded, plain)
+        sums = [jnp.sum(value, axis=0, keepdims=True) for value in sums]
+        sums = jnp.concatenate(sums + [jnp.zeros((BACK - 6, 128), F32)], axis=0)
+        groups.append(jnp.where(row + n * 128.0 < runs[...], sums, 0.0))
+    return jnp.concatenate(groups, axis=1)
+
+
+def send_back(red, perm, runs, largest, a_s, w_s, col, tg, later, sent, red_last, sums_s):
+    last = QUADS - 1
+    for at in range(last):
+        sums_s[at] = reduced(red.at[at], runs.at[at])
+    backward_whole(
+        runs.at[last], a_s, w_s, col, tg, later, red_last
+    )
+    sums = [sums_s[at] for at in range(last)] + [reduced(red_last, runs.at[last])]
+    swap = [largest[:, 0:1] == float(q) for q in range(last)]
+    moved = sums[last]
+    for q in range(last):
+        moved = jnp.where(swap[q], sums[q], moved)
+    sums = [jnp.where(swap[q], sums[last], sums[q]) for q in range(last)] + [moved]
+    parts = [jnp.concatenate(three_parts(p), axis=0).astype(BF16) for p in sums]
+    placed = [jnp.dot(p, perm[q], preferred_element_type=F32) for q, p in enumerate(parts)]
+    placed = [(p[2 * BACK :] + p[BACK : 2 * BACK]) + p[0:BACK] for p in placed]
+    back = [jnp.concatenate([p[:, c * GS : (c + 1) * GS] for c in range(CAP)], axis=0).T for p in placed]
     for j in range(QUADS // 2):
         sent[:, j, :] = jnp.concatenate([back[2 * j], back[2 * j + 1]], axis=1)
 
 
 def unpack_kernel(
-    red_ref, perm_ref, runs_ref, own_ref, angles_ref, parts_ref, move_ref, basis_ref,
-    sent_ref, back, ret_ref, part_ref, sems
+    red, perm, runs, largest, a_s, w_s, col, tg, later, own_ref, angles_ref, parts_ref, move_ref, basis_ref,
+    sent_ref, red_last, sums_s, ret_ref, part_ref, sems
 ):
     greet()
     me, view = peers()
-    send_back(red_ref, perm_ref, runs_ref, sent_ref, back)
+    send_back(red, perm, runs, largest, a_s, w_s, col, tg, later, sent_ref, red_last, sums_s)
     ret_ref[me] = sent_ref[me]
     slot = own_ref[0:1, :].astype(jnp.int32)
     owner = jnp.where(iota((GS, G), 0) == (slot >> 5), 1.0, 0.0).astype(BF16)
     owner = jnp.concatenate([owner] * 3, axis=0)
     place = slot & 31
-    total = jnp.zeros((BACK, G), F32)
     greeted()
     deal(sent_ref, ret_ref, sems.at[0], sems.at[1])
     polar = jnp.concatenate([angles_ref[v, 0:1, :] for v in range(VIEWS)], axis=0)
@@ -491,13 +523,14 @@
     for k, values in enumerate(sh_basis(polar, azimuth)):
         basis_ref[k] = values
     settle(ret_ref, GS - 1, sems.at[1])
-    for j in range(QUADS // 2):
-        parts = jnp.concatenate(three_parts(ret_ref[:, j, :]), axis=0).astype(BF16)
-        spread = lax.dot_general(
-            parts, owner, (((0,), (0,)), ((), ())), preferred_element_type=F32
-        )
-        for i in range(16):
-            total = jnp.where(place == j * 16 + i, spread[i * BACK : (i + 1) * BACK, :], total)
+    both = jnp.concatenate([ret_ref[:, j, :] for j in range(QUADS // 2)], axis=1)
+    parts = jnp.concatenate(three_parts(both), axis=0).astype(BF16)
+    spread = lax.dot_general(parts, owner, (((0,), (0,)), ((), ())), preferred_element_type=F32)
+    found = [spread[i * BACK : (i + 1) * BACK, :] for i in range(QUADS * CAP)]
+    for bit in range(5):
+        odd = ((place >> bit) & 1) == 1
+        found = [jnp.where(odd, found[i + 1], found[i]) for i in range(0, len(found), 2)]
+    total = found[0]
     m, n, a, b, c = (own_ref[k : k + 1, :] for k in range(1, 6))
     plain = total[5:6, :]
     du = total[3:4, :] - m * plain
@@ -574,41 +607,48 @@
         ins,
         [
             (3, QUADS, PIX),
-            (QUADS, PLACES, 5 * 128),
+            (QUADS - 1, PLACES, 5 * 128),
             jax.ShapeDtypeStruct((QUADS, PLACES, PLACES), BF16),
             (QUADS, 8, 128),
+            (8, 128),
+            (PLACES, PIX),
+            (PLACES, PIX),
+            (PLACES, 3 * 128),
+            (3, 8, PIX),
+            (8, PIX),
         ],
         [
             pltpu.VMEM((QUADS, PLACES, FORMS * 128), F32),
-            pltpu.VMEM((QUADS, PLACES, PIX), F32),
-            pltpu.VMEM((QUADS, PLACES, PIX), F32),
+            pltpu.VMEM((QUADS - 1, PLACES, PIX), F32),
+            pltpu.VMEM((QUADS - 1, PLACES, PIX), F32),
+            pltpu.VMEM((QUADS - 1, 3, 8, PIX), F32),
+            pltpu.VMEM((QUADS - 1, 8, PIX), F32),
             pltpu.VMEM((QUADS, 8, PIX), F32),
             pltpu.VMEM((QUADS, 3, 8, PIX), F32),
-            pltpu.VMEM((QUADS, 3, 8, PIX), F32),
-            pltpu.VMEM((QUADS, 8, PIX), F32),
             pltpu.VMEM((QUADS, 24, 128), F32),
             pltpu.VMEM((QUADS, 24, 128), F32),
             pltpu.VMEM((QUADS, GS, 128), F32),
             pltpu.VMEM((QUADS, 3, PIX), F32),
             pltpu.SMEM((QUADS,), jnp.int32),
         ],
-        limit=44,
-    )
-
-
-def unpack(sums, perm, runs, own, angles):
+        limit=RENDER_MIB,
+    )
+
+
+def unpack(*ins):
     return call(
         unpack_kernel,
-        [sums, perm, runs, own, angles],
+        ins,
         [(VIEWS, 4, G), (2, G), (16, VIEWS, G)],
         [
             pltpu.VMEM((GS, QUADS // 2, 128), F32),
-            pltpu.VMEM((QUADS, GS, GS), F32),
+            pltpu.VMEM((PLACES, 5 * 128), F32),
+            pltpu.VMEM((QUADS - 1, BACK, PLACES), F32),
             pltpu.VMEM((GS, QUADS // 2, 128), F32),
             pltpu.VMEM((4, G), F32),
             pltpu.SemaphoreType.DMA((4,)),
         ],
-        limit=24,
+        limit=UNPACK_MIB,
         remote=1,
     )
 
@@ -628,8 +668,8 @@
         depth_rank,
         jnp.transpose(target[0], (1, 0, 2)),
     )
-    images, sums, perm, runs = render(arrived, *prepared)
-    parts, move, basis = unpack(sums, perm, runs, own, angles)
+    images, *blended = render(arrived, *prepared)
+    parts, move, basis = unpack(*blended, own, angles)
     sh_grad, logit_grad, mean_grad = final(parts, move, basis, own)
     return (sh_grad, logit_grad.reshape(G), mean_grad[None], jnp.transpose(images, (1, 0, 2))[None])
 

time: 42.1 us -> 41.5 us (0.986)
  Pallas kernels: 41.4 us -> 40.8 us
    pallas_call x4, Pallas kernels: 41.4 us -> 40.8 us  [call(): pl.pallas_call(kernel, out_shape=shapes, in_specs=[pl.BlockSpec(memory_sp...]
where the time goes in v5:
time: 41.5 us; the launch traced here: 41.4 us
  Pallas kernels  40.8 us (98%)
  between operations  0.65 us (2%)
    pallas_call x4, Pallas kernels, call(): pl.pallas_call(kernel, out_shape=shapes, in_specs=[pl.BlockSpec(memory_sp...  40.8 us

profile of v5, /device:TPU:1, one launch (start us, length us, event | category | flops | bytes accessed | tf_op | source)
XLA Modules:
  0.0 41.4 jit_solution(12512785572688039615)
XLA Ops:
  0.6 16.5 %shard_map.111 = (f32[64,4,128]{2,1,0:T(4,128)S(1)}, f32[4,2,1024]{2,1,0:T(2,128)S(1)}, f32[7,1024]{1,0:T(8,128)S(1)}, f32[4,24,128]{2,1,0:T(8,128)S(1)}, bf16[6...) custom-call(f32[48,1024]{1,0:T(8,128)} %refs_0_.1, f32[1,1024]{1,0:T(1,128)} %bitcast.16, ...), custom_call_target="tpu_custom_call" | custom-call | tf_op jit(solution)/shard_map/pallas_call | solution.py:569
  17.2 7.8 %shard_map.112 = (f32[3,4,1024]{2,1,0:T(4,128)}, f32[3,512,640]{2,1,0:T(8,128)S(1)}, bf16[4,512,512]{2,1,0:T(8,128)(2,1)S(1)}, f32[4,8,128]{2,1,0:T(8,128)S(1)},...) custom-call(f32[64,4,128]{2,1,0:T(4,128)S(1)} %get-tuple-element.27., ...), custom_call_target="tpu_custom_call" | custom-call | tf_op jit(solution)/shard_map/pallas_call | solution.py:569
  25.0 15.6 %shard_map.113 = (f32[4,4,1024]{2,1,0:T(4,128)S(1)}, f32[2,1024]{1,0:T(2,128)S(1)}, f32[16,4,1024]{2,1,0:T(4,128)S(1)}) custom-call(f32[3,512,640]{2,1,0:T(8,128)S(1)} %get-tuple-element.32.red, bf16[4,512,512]{2,1,0:T(8,128)(2,1)S(1)} %get-tuple-element.33.perm, f32[4,8,128]{2,1,0:T(8,128)S(1)} %get-tuple-element.34.runs, ...), custom_call_target="tpu_custom_call" | custom-call | tf_op jit(solution)/shard_map/pallas_call | solution.py:569
  40.6 0.8 %shard_map.114 = (f32[48,1024]{1,0:T(8,128)}, f32[1,1024]{1,0:T(1,128)}, f32[2,1024]{1,0:T(2,128)}) custom-call(f32[4,4,1024]{2,1,0:T(4,128)S(1)} %get-tuple-element.43.part_ref, f32[2,1024]{1,0:T(2,128)S(1)} %get-tuple-element.44.move_ref, f32[16,4,1024]{2,1,0:T(4,128)S(1)} %get-tuple-element.45.basis_ref, f32[7,1024]{1,0:T(8,128)S(1)} %get-tuple-element.41.own_ref), custom_call_target="tpu_custom_call" | custom-call | tf_op jit(solution)/shard_map/pallas_call | solution.py:569

commit v6 on v5

--- a/solution.py
+++ b/solution.py
@@ -39,6 +39,8 @@
 TILES = PIX // 128
 WIDE = 16
 COL, KEY = 6, 9
+SENT = 12
+ROWS = QUADS * CAP * SENT // 128
 BACK = 8
 OWN = 7
 SHIFT = 64.0
@@ -175,7 +177,7 @@
     scale = LOG2E / 1024.0
     opacity = 0.99 * jax.nn.sigmoid(logit_ref[...])
     a, b, c = (conic_ref[k] * scale for k in range(3))
-    pay[...] = jnp.zeros((WIDE, G), F32)
+    pay[...] = jnp.zeros((SENT, G), F32)
     away = 0.5 * (a * m * m + 2.0 * b * m * n + c * n * n)
     pay[0:1, :] = (jnp.log(opacity) * LOG2E + SHIFT) - away
     pay[1:2, :] = a * m + b * n
@@ -188,17 +190,18 @@
     parts = three_parts(pay[...])
     slot = slot_ref[...]
     owner = jnp.where(iota((GS, G), 0) == (slot >> 5), 1.0, 0.0).astype(BF16)
-    place = slot & 31
-    for q in range(QUADS):
-        total = jnp.zeros((GS, 128), F32)
-        for part in parts[::-1]:
-            spread = jnp.concatenate(
-                [jnp.where(place == q * CAP + cap, part, 0.0) for cap in range(CAP)], axis=0
-            ).astype(BF16)
-            total = total + lax.dot_general(
-                owner, spread, (((1,), (1,)), ((), ())), preferred_element_type=F32
-            )
-        out_ref[:, q, :] = total
+    place = (slot & 31) - jnp.where(iota((2 * SENT, G), 0) >= SENT, 1, 0)
+    total = jnp.zeros((GS, ROWS * 128), F32)
+    for part in parts[::-1]:
+        pair = jnp.concatenate([part, part], axis=0)
+        spread = jnp.concatenate(
+            [jnp.where(place == i, pair, 0.0) for i in range(0, QUADS * CAP, 2)], axis=0
+        ).astype(BF16)
+        total = total + lax.dot_general(
+            owner, spread, (((1,), (1,)), ((), ())), preferred_element_type=F32
+        )
+    for r in range(ROWS):
+        out_ref[:, r, :] = total[:, tile(r)]
     arr_ref[me] = out_ref[me]
     mono[...] = monomials()
     at = iota((PLACES, 128), 0)
@@ -208,6 +211,11 @@
         for c in range(3):
             for t in range(TILES):
                 tgt[q, c * 8 + t : c * 8 + t + 1, :] = tgt_ref[c, q : q + 1, tile(t)]
+    for q in range(QUADS):
+        y = tgt[q, 0:24, :]
+        means = window_means(jnp.concatenate([y, y * y], axis=0))
+        tgt[q, 24:48, :] = means[0:24]
+        tgt[q, 48:72, :] = means[24:48] - means[0:24] * means[0:24]
     greeted()
     deal(out_ref, arr_ref, sems.at[0], sems.at[1])
     spread_views(angle_ref, angles_ref, sems.at[2], sems.at[3])
@@ -249,22 +257,26 @@
     return jnp.concatenate([base, base, base, shift], axis=0).astype(BF16)
 
 
-def loss_slope(x, y):
+def window_means(values):
     lane = iota((128, 128), 1)
     other = iota((128, 128), 0)
     same = ((lane & 31) >> 2) == ((other & 31) >> 2)
     pool = jnp.where(same, 1.0 / 16.0, 0.0).astype(BF16)
+    rows = values.shape[0]
+    sums = jnp.dot(
+        jnp.concatenate(three_parts(values), axis=0).astype(BF16), pool, preferred_element_type=F32
+    )
+    return (sums[2 * rows :] + sums[rows : 2 * rows]) + sums[0:rows]
+
+
+def loss_slope(x, y, my, vy):
     rows = x.shape[0]
-    parts = three_parts(jnp.concatenate([x, y, x * x, y * y, x * y], axis=0))
-    sums = jnp.dot(
-        jnp.concatenate(parts, axis=0).astype(BF16), pool, preferred_element_type=F32
-    )
-    means = (sums[10 * rows : 15 * rows] + sums[5 * rows : 10 * rows]) + sums[0 : 5 * rows]
-    mx, my, exx, eyy, exy = (means[k * rows : (k + 1) * rows] for k in range(5))
+    means = window_means(jnp.concatenate([x, x * x, x * y], axis=0))
+    mx, exx, exy = (means[k * rows : (k + 1) * rows] for k in range(3))
     n1 = 2.0 * mx * my + SSIM_MEAN
     n2 = 2.0 * (exy - mx * my) + SSIM_SPREAD
     d1 = mx * mx + my * my + SSIM_MEAN
-    d2 = (exx - mx * mx) + (eyy - my * my) + SSIM_SPREAD
+    d2 = (exx - mx * mx) + vy + SSIM_SPREAD
     i1, i2 = 1.0 / d1, 1.0 / d2
     both = i1 * i2
     ratio = n1 * n2 * both
@@ -280,12 +292,14 @@
     return jnp.where(keep, pltpu.roll(values, by % 8, 0), fill)
 
 
-def order(blocks, xs, perm, bc, mono, step_s, sub_s):
+def order(blocks, arrived, perm, bc, mono, step_s, sub_s):
     pick = jnp.where((iota((3 * WIDE, 128), 0) & 15) == KEY, 1.0, 0.0).astype(BF16)
-    turned = [x.T for x in xs]
-    packed = [
-        jnp.concatenate([t[c * WIDE : (c + 1) * WIDE, :] for c in range(CAP)], axis=1) for t in turned
-    ]
+    turned = jnp.concatenate([arrived[:, r, :].T for r in range(ROWS)], axis=0)
+    rest = jnp.zeros((WIDE - SENT, PLACES), F32)
+    packed = []
+    for q in blocks:
+        places = [turned[i * SENT : (i + 1) * SENT, :] for i in range(q * CAP, (q + 1) * CAP)]
+        packed.append(jnp.concatenate([jnp.concatenate(places, axis=1), rest], axis=0))
     parts = [jnp.concatenate(three_parts(p), axis=0).astype(BF16) for p in packed]
     keys = [p[KEY : KEY + 1, :] for p in packed]
     columns = [
@@ -412,7 +426,7 @@
         image[c : c + 1, :] = row
         for t in range(TILES):
             pic[c * 8 + t : c * 8 + t + 1, :] = row[:, tile(t)]
-    slope[...] = loss_slope(pic[...], tgt[...])
+    slope[...] = loss_slope(pic[...], *(tgt[24 * k : 24 * k + 24, :] for k in range(3)))
     behind = jnp.zeros((8, PIX), F32)
     for c in range(3):
         row = jnp.concatenate([slope[c * 8 + t : c * 8 + t + 1, :] for t in range(TILES)], axis=1)
@@ -428,11 +442,9 @@
 def render_kernel(
     arr_ref, tgt, mono, step_s, sub_s,
     img_ref, red, perm, runs, largest, a_last, w_last, col_last, tg_last, later_last,
-    bc, a_s, w_s, tg, later, left, seen, pic, slope, xq, image, runs_s
+    bc, a_s, w_s, tg, later, left, seen, pic, slope, image, runs_s
 ):
-    for q in range(QUADS):
-        xq[q] = arr_ref[:, q, :]
-    found = order(list(range(QUADS)), [xq[q] for q in range(QUADS)], perm, bc, mono, step_s, sub_s)
+    found = order(list(range(QUADS)), arr_ref, perm, bc, mono, step_s, sub_s)
     for q, turn in enumerate(found):
         runs_s[q] = jnp.sum(turn).astype(jnp.int32) * UNROLL
     best = jnp.int32(0)
@@ -472,15 +484,25 @@
     pixel = iota((128, 128), 0)
     across = ((pixel & 31) - 16).astype(F32)
     down = ((pixel >> 5) - 16).astype(F32)
-    row = iota((BACK, 128), 1).astype(F32)
+    row = iota((BACK, PLACES), 1).astype(F32)
+    colour = red[:, 0 : 3 * 128]
+    high = colour.astype(BF16)
+    low = (colour - high.astype(F32)).astype(BF16)
+    pick = jnp.where(iota((BACK, 3 * 128), 1) >> 7 == iota((BACK, 3 * 128), 0), 1.0, 0.0).astype(BF16)
+    nt = (((1,), (1,)), ((), ()))
+    sums = lax.dot_general(pick, low, nt, preferred_element_type=F32) + lax.dot_general(
+        pick, high, nt, preferred_element_type=F32
+    )
     groups = []
     for n in range(PLACES // 128):
-        g0, g1, g2, plain, graded = (red[tile(n), tile(k)].T for k in range(5))
-        sums = (g0, g1, g2, plain * across, plain * down + 4.0 * graded, plain)
-        sums = [jnp.sum(value, axis=0, keepdims=True) for value in sums]
-        sums = jnp.concatenate(sums + [jnp.zeros((BACK - 6, 128), F32)], axis=0)
-        groups.append(jnp.where(row + n * 128.0 < runs[...], sums, 0.0))
-    return jnp.concatenate(groups, axis=1)
+        plain, graded = (red[tile(n), tile(k)].T for k in (3, 4))
+        moved = (plain * across, plain * down + 4.0 * graded, plain)
+        moved = [jnp.sum(value, axis=0, keepdims=True) for value in moved]
+        groups.append(jnp.concatenate(moved, axis=0))
+    sums = jnp.concatenate(
+        [sums[0:3], jnp.concatenate(groups, axis=1), jnp.zeros((BACK - 6, PLACES), F32)], axis=0
+    )
+    return jnp.where(row < runs[0:1, 0:1], sums, 0.0)
 
 
 def send_back(red, perm, runs, largest, a_s, w_s, col, tg, later, sent, red_last, sums_s):
@@ -546,8 +568,9 @@
     settle(parts_ref, VIEWS - 1, sems.at[2])
 
 
-def final_kernel(part_ref, move_ref, basis_ref, own_ref, sh_ref, logit_grad_ref, mean_grad_ref):
+def final_kernel(part_ref, move_ref, basis_ref, own_ref, image_ref, sh_ref, logit_grad_ref, mean_grad_ref, img_ref):
     mean_grad_ref[...] = move_ref[...]
+    img_ref[...] = image_ref[...]
     plain = part_ref[0, 3:4, :]
     for v in range(1, VIEWS):
         plain = plain + part_ref[v, 3:4, :]
@@ -581,18 +604,18 @@
         pack_kernel,
         [pltpu.with_memory_space_constraint(i, pltpu.HBM) for i in ins],
         [
-            (GS, QUADS, 128),
+            (GS, ROWS, 128),
             (VIEWS, 2, G),
             (OWN, G),
-            (QUADS, 24, 128),
+            (QUADS, 72, 128),
             jax.ShapeDtypeStruct((4 * WIDE, FORMS * 128), BF16),
             (PLACES, 128),
             (PLACES, 128),
         ],
         [pltpu.VMEM(i.shape, i.dtype) for i in ins]
         + [
-            pltpu.VMEM((GS, QUADS, 128), F32),
-            pltpu.VMEM((WIDE, G), F32),
+            pltpu.VMEM((GS, ROWS, 128), F32),
+            pltpu.VMEM((SENT, G), F32),
             pltpu.SemaphoreType.DMA((4,)),
             pltpu.SemaphoreType.DMA((len(ins),)),
         ],
@@ -627,7 +650,6 @@
             pltpu.VMEM((QUADS, 3, 8, PIX), F32),
             pltpu.VMEM((QUADS, 24, 128), F32),
             pltpu.VMEM((QUADS, 24, 128), F32),
-            pltpu.VMEM((QUADS, GS, 128), F32),
             pltpu.VMEM((QUADS, 3, PIX), F32),
             pltpu.SMEM((QUADS,), jnp.int32),
         ],
@@ -654,7 +676,7 @@
 
 
 def final(*ins):
-    return call(final_kernel, ins, [(48, G), (1, G), (2, G)])
+    return call(final_kernel, ins, [(48, G), (1, G), (2, G), (3, QUADS, PIX)])
 
 
 def local(sh_coef, opacity_logit, view_angle, mean_pos, conic, send_slot, depth_rank, target):
@@ -670,7 +692,7 @@
     )
     images, *blended = render(arrived, *prepared)
     parts, move, basis = unpack(*blended, own, angles)
-    sh_grad, logit_grad, mean_grad = final(parts, move, basis, own)
+    sh_grad, logit_grad, mean_grad, images = final(parts, move, basis, own, images)
     return (sh_grad, logit_grad.reshape(G), mean_grad[None], jnp.transpose(images, (1, 0, 2))[None])
 
 

time: 41.5 us -> 40.7 us (0.981)
  Pallas kernels: 40.8 us -> 39.9 us
    pallas_call x4, Pallas kernels: 40.8 us -> 39.9 us  [call(): pl.pallas_call(kernel, out_shape=shapes, in_specs=[pl.BlockSpec(memory_sp...]
where the time goes in v6:
time: 40.7 us; the launch traced here: 40.5 us
  Pallas kernels  39.9 us (98%)
  between operations  0.66 us (2%)
    pallas_call x4, Pallas kernels, call(): pl.pallas_call(kernel, out_shape=shapes, in_specs=[pl.BlockSpec(memory_sp...  39.9 us

profile of v6, /device:TPU:1, one launch (start us, length us, event | category | flops | bytes accessed | tf_op | source)
XLA Modules:
  0.0 40.5 jit_solution(10818815188258565359)
XLA Ops:
  0.6 16.2 %shard_map.111 = (f32[64,3,128]{2,1,0:T(4,128)S(1)}, f32[4,2,1024]{2,1,0:T(2,128)S(1)}, f32[7,1024]{1,0:T(8,128)S(1)}, f32[4,72,128]{2,1,0:T(8,128)S(1)}, bf16[6...) custom-call(f32[48,1024]{1,0:T(8,128)} %refs_0_.1, f32[1,1024]{1,0:T(1,128)} %bitcast.16, ...), custom_call_target="tpu_custom_call" | custom-call | tf_op jit(solution)/shard_map/pallas_call | solution.py:592
  16.9 7.4 %shard_map.112 = (f32[3,4,1024]{2,1,0:T(4,128)S(1)}, f32[3,512,640]{2,1,0:T(8,128)S(1)}, bf16[4,512,512]{2,1,0:T(8,128)(2,1)S(1)}, f32[4,8,128]{2,1,0:T(8,128)S(...) custom-call(f32[64,3,128]{2,1,0:T(4,128)S(1)} %get-tuple-element.28., ...), custom_call_target="tpu_custom_call" | custom-call | tf_op jit(solution)/shard_map/pallas_call | solution.py:592
  24.2 15.5 %shard_map.113 = (f32[4,4,1024]{2,1,0:T(4,128)S(1)}, f32[2,1024]{1,0:T(2,128)S(1)}, f32[16,4,1024]{2,1,0:T(4,128)S(1)}) custom-call(f32[3,512,640]{2,1,0:T(8,128)S(1)} %get-tuple-element.33.red, bf16[4,512,512]{2,1,0:T(8,128)(2,1)S(1)} %get-tuple-element.34.perm, f32[4,8,128]{2,1,0:T(8,128)S(1)} %get-tuple-element.35.runs, ...), custom_call_target="tpu_custom_call" | custom-call | tf_op jit(solution)/shard_map/pallas_call | solution.py:592
  39.7 0.8 %shard_map.114 = (f32[48,1024]{1,0:T(8,128)}, f32[1,1024]{1,0:T(1,128)}, f32[2,1024]{1,0:T(2,128)}, f32[3,4,1024]{2,1,0:T(4,128)}) custom-call(f32[4,4,1024]{2,1,0:T(4,128)S(1)} %get-tuple-element.44.part_ref, f32[2,1024]{1,0:T(2,128)S(1)} %get-tuple-element.45.move_ref, f32[16,4,1024]{2,1,0:T(4,128)S(1)} %get-tuple-element.46.basis_ref, ...), custom_call_target="tpu_custom_call" | custom-call | tf_op jit(solution)/shard_map/pallas_call | solution.py:592

commit v7 on v6

--- a/solution.py
+++ b/solution.py
@@ -107,10 +107,13 @@
     return [across[x] + along[z] + core[c] for x, z, c in steps if (x, z, c) != (0, 0, 0)]
 
 
-def greet():
+def greet(between=()):
     me, view = peers()
     barrier = pltpu.get_barrier_semaphore()
-    for other in far_first(me):
+    for n, other in enumerate(far_first(me)):
+        if n == 16:
+            for copy in between:
+                copy.start()
         pl.semaphore_signal(barrier, inc=1, device_id=(other, view), device_id_type=MESH)
     for d in range(1, VIEWS):
         pl.semaphore_signal(barrier, inc=1, device_id=(me, lax.rem(view + d, VIEWS)), device_id_type=MESH)
@@ -135,7 +138,7 @@
 
 def spread_views(mine, got, send_sem, recv_sem):
     me, view = peers()
-    for d in range(1, VIEWS):
+    for d in (2, 1, 3):
         pltpu.make_async_remote_copy(
             src_ref=mine,
             dst_ref=got.at[view],
@@ -158,9 +161,7 @@
     loads = [
         pltpu.make_async_copy(src, dst, load_sems.at[k]) for k, (src, dst) in enumerate(zip(far, near))
     ]
-    greet()
-    for load in loads:
-        load.start()
+    greet(loads)
     for load in loads:
         load.wait()
     sh_ref, logit_ref, angle_ref, mean_ref, conic_ref, slot_ref, rank_ref, tgt_ref = near
@@ -543,7 +544,8 @@
     polar = jnp.concatenate([angles_ref[v, 0:1, :] for v in range(VIEWS)], axis=0)
     azimuth = jnp.concatenate([angles_ref[v, 1:2, :] for v in range(VIEWS)], axis=0)
     for k, values in enumerate(sh_basis(polar, azimuth)):
-        basis_ref[k] = values
+        for v in range(VIEWS):
+            basis_ref[v, 3 * k : 3 * k + 3, :] = jnp.broadcast_to(values[v : v + 1, :], (3, G))
     settle(ret_ref, GS - 1, sems.at[1])
     both = jnp.concatenate([ret_ref[:, j, :] for j in range(QUADS // 2)], axis=1)
     parts = jnp.concatenate(three_parts(both), axis=0).astype(BF16)
@@ -575,11 +577,12 @@
     for v in range(1, VIEWS):
         plain = plain + part_ref[v, 3:4, :]
     logit_grad_ref[...] = plain * (1.0 - jax.nn.sigmoid(own_ref[6:7, :]))
-    for k in range(16):
-        total = part_ref[0, 0:3, :] * basis_ref[k, 0:1, :]
+    colours = [jnp.concatenate([part_ref[v, 0:3, :]] * 8, axis=0) for v in range(VIEWS)]
+    for half in (slice(0, 24), slice(24, 48)):
+        total = colours[0] * basis_ref[0, half, :]
         for v in range(1, VIEWS):
-            total = total + part_ref[v, 0:3, :] * basis_ref[k, v : v + 1, :]
-        sh_ref[3 * k : 3 * k + 3, :] = total
+            total = total + colours[v] * basis_ref[v, half, :]
+        sh_ref[half, :] = total
 
 
 MESH = pl.DeviceIdType.MESH
@@ -661,7 +664,7 @@
     return call(
         unpack_kernel,
         ins,
-        [(VIEWS, 4, G), (2, G), (16, VIEWS, G)],
+        [(VIEWS, 4, G), (2, G), (VIEWS, 48, G)],
         [
             pltpu.VMEM((GS, QUADS // 2, 128), F32),
             pltpu.VMEM((PLACES, 5 * 128), F32),

time: 40.7 us -> 40.6 us (level)
  no operation moved by 1% of the time
where the time goes in v7:
time: 40.6 us; the launch traced here: 40.7 us
  Pallas kernels  40 us (99%)
  between operations  0.66 us (2%)
    pallas_call x4, Pallas kernels, call(): pl.pallas_call(kernel, out_shape=shapes, in_specs=[pl.BlockSpec(memory_sp...  40 us

profile of v7, /device:TPU:1, one launch (start us, length us, event | category | flops | bytes accessed | tf_op | source)
XLA Modules:
  0.0 40.7 jit_solution(4036965017422436464)
XLA Ops:
  0.6 16.3 %shard_map.111 = (f32[64,3,128]{2,1,0:T(4,128)S(1)}, f32[4,2,1024]{2,1,0:T(2,128)S(1)}, f32[7,1024]{1,0:T(8,128)S(1)}, f32[4,72,128]{2,1,0:T(8,128)S(1)}, bf16[6...) custom-call(f32[48,1024]{1,0:T(8,128)} %refs_0_.1, f32[1,1024]{1,0:T(1,128)} %bitcast.16, ...), custom_call_target="tpu_custom_call" | custom-call | tf_op jit(solution)/shard_map/pallas_call | solution.py:595
  16.9 7.9 %shard_map.112 = (f32[3,4,1024]{2,1,0:T(4,128)S(1)}, f32[3,512,640]{2,1,0:T(8,128)S(1)}, bf16[4,512,512]{2,1,0:T(8,128)(2,1)S(1)}, f32[4,8,128]{2,1,0:T(8,128)S(...) custom-call(f32[64,3,128]{2,1,0:T(4,128)S(1)} %get-tuple-element.28., ...), custom_call_target="tpu_custom_call" | custom-call | tf_op jit(solution)/shard_map/pallas_call | solution.py:595
  24.8 15.0 %shard_map.113 = (f32[4,4,1024]{2,1,0:T(4,128)S(1)}, f32[2,1024]{1,0:T(2,128)S(1)}, f32[4,48,1024]{2,1,0:T(8,128)S(1)}) custom-call(f32[3,512,640]{2,1,0:T(8,128)S(1)} %get-tuple-element.33.red, bf16[4,512,512]{2,1,0:T(8,128)(2,1)S(1)} %get-tuple-element.34.perm, f32[4,8,128]{2,1,0:T(8,128)S(1)} %get-tuple-element.35.runs, ...), custom_call_target="tpu_custom_call" | custom-call | tf_op jit(solution)/shard_map/pallas_call | solution.py:595
  39.8 0.8 %shard_map.114 = (f32[48,1024]{1,0:T(8,128)}, f32[1,1024]{1,0:T(1,128)}, f32[2,1024]{1,0:T(2,128)}, f32[3,4,1024]{2,1,0:T(4,128)}) custom-call(f32[4,4,1024]{2,1,0:T(4,128)S(1)} %get-tuple-element.44.part_ref, f32[2,1024]{1,0:T(2,128)S(1)} %get-tuple-element.45.move_ref, f32[4,48,1024]{2,1,0:T(8,128)S(1)} %get-tuple-element.46.basis_ref, ...), custom_call_target="tpu_custom_call" | custom-call | tf_op jit(solution)/shard_map/pallas_call | solution.py:595

commit v8 on v7

--- a/solution.py
+++ b/solution.py
@@ -491,8 +491,11 @@
     low = (colour - high.astype(F32)).astype(BF16)
     pick = jnp.where(iota((BACK, 3 * 128), 1) >> 7 == iota((BACK, 3 * 128), 0), 1.0, 0.0).astype(BF16)
     nt = (((1,), (1,)), ((), ()))
-    sums = lax.dot_general(pick, low, nt, preferred_element_type=F32) + lax.dot_general(
-        pick, high, nt, preferred_element_type=F32
+    sums = lax.dot_general(
+        jnp.concatenate([pick, pick], axis=1),
+        jnp.concatenate([low, high], axis=1),
+        nt,
+        preferred_element_type=F32,
     )
     groups = []
     for n in range(PLACES // 128):

time: 40.6 us -> 40.8 us (level)
  no operation moved by 1% of the time
where the time goes in v8:
time: 40.8 us; the launch traced here: 40.6 us
  Pallas kernels  39.9 us (98%)
  between operations  0.66 us (2%)
    pallas_call x4, Pallas kernels, call(): pl.pallas_call(kernel, out_shape=shapes, in_specs=[pl.BlockSpec(memory_sp...  39.9 us

profile of v8, /device:TPU:1, one launch (start us, length us, event | category | flops | bytes accessed | tf_op | source)
XLA Modules:
  0.0 40.6 jit_solution(14719601855185639241)
XLA Ops:
  0.6 16.3 %shard_map.111 = (f32[64,3,128]{2,1,0:T(4,128)S(1)}, f32[4,2,1024]{2,1,0:T(2,128)S(1)}, f32[7,1024]{1,0:T(8,128)S(1)}, f32[4,72,128]{2,1,0:T(8,128)S(1)}, bf16[6...) custom-call(f32[48,1024]{1,0:T(8,128)} %refs_0_.1, f32[1,1024]{1,0:T(1,128)} %bitcast.16, ...), custom_call_target="tpu_custom_call" | custom-call | tf_op jit(solution)/shard_map/pallas_call | solution.py:598
  16.9 7.6 %shard_map.112 = (f32[3,4,1024]{2,1,0:T(4,128)S(1)}, f32[3,512,640]{2,1,0:T(8,128)S(1)}, bf16[4,512,512]{2,1,0:T(8,128)(2,1)S(1)}, f32[4,8,128]{2,1,0:T(8,128)S(...) custom-call(f32[64,3,128]{2,1,0:T(4,128)S(1)} %get-tuple-element.28., ...), custom_call_target="tpu_custom_call" | custom-call | tf_op jit(solution)/shard_map/pallas_call | solution.py:598
  24.5 15.2 %shard_map.113 = (f32[4,4,1024]{2,1,0:T(4,128)S(1)}, f32[2,1024]{1,0:T(2,128)S(1)}, f32[4,48,1024]{2,1,0:T(8,128)S(1)}) custom-call(f32[3,512,640]{2,1,0:T(8,128)S(1)} %get-tuple-element.33.red, bf16[4,512,512]{2,1,0:T(8,128)(2,1)S(1)} %get-tuple-element.34.perm, f32[4,8,128]{2,1,0:T(8,128)S(1)} %get-tuple-element.35.runs, ...), custom_call_target="tpu_custom_call" | custom-call | tf_op jit(solution)/shard_map/pallas_call | solution.py:598
  39.7 0.8 %shard_map.114 = (f32[48,1024]{1,0:T(8,128)}, f32[1,1024]{1,0:T(1,128)}, f32[2,1024]{1,0:T(2,128)}, f32[3,4,1024]{2,1,0:T(4,128)}) custom-call(f32[4,4,1024]{2,1,0:T(4,128)S(1)} %get-tuple-element.44.part_ref, f32[2,1024]{1,0:T(2,128)S(1)} %get-tuple-element.45.move_ref, f32[4,48,1024]{2,1,0:T(8,128)S(1)} %get-tuple-element.46.basis_ref, ...), custom_call_target="tpu_custom_call" | custom-call | tf_op jit(solution)/shard_map/pallas_call | solution.py:598
